TPU v7x, 32 devices: a whole 2x2x4 slice. The times are simulated.
32 devices in a mesh: group: 4 (over z), replica: 8 (over y, x, core).
Axes of the slice: x: 2, y: 2, z: 4, core: 2. Of those that a mesh axis runs over, the one named last changes fastest.
Arguments:
- hidden_in: bfloat16 [8192, 640], P(('group', 'replica')), may hold values from -63 to 63, as said below
- cotangent: bfloat16 [8192, 640], P(('group', 'replica')), may hold values from -15 to 15, as said below
- segment_ids: int32 [8192], P(('group', 'replica')), may hold values from 0 to 1, as said below
- positions: int32 [8192], P(('group', 'replica')), may hold values from 0 to 16382, as said below
- w_qkv: bfloat16 [640, 1536], P('group'), may hold values from -0.25 to 0.25
- w_out: bfloat16 [1024, 640], P('group'), may hold values from -0.1875 to 0.1875
- w_gate_up: bfloat16 [640, 4096], P('group'), may hold values from -0.25 to 0.25
- w_down: bfloat16 [2048, 640], P('group'), may hold values from -0.125 to 0.125
- norm_gains: float32 [3072], replicated, may hold values from -0.08 to 0.08
- first_qkv: float32 [640, 1536], P('group', 'replica'), may hold values from -128 to 128
- first_out: float32 [1024, 640], P('group', 'replica'), may hold values from -128 to 128
- first_gate_up: float32 [640, 4096], P('group', 'replica'), may hold values from -128 to 128
- first_down: float32 [2048, 640], P('group', 'replica'), may hold values from -128 to 128
- first_gains: float32 [3072], P(('group', 'replica')), may hold values from -128 to 128
- second_qkv: float32 [640, 1536], P('group', 'replica'), may hold values from 16.384 to 262.144
- second_out: float32 [1024, 640], P('group', 'replica'), may hold values from 16.384 to 262.144
- second_gate_up: float32 [640, 4096], P('group', 'replica'), may hold values from 16.384 to 262.144
- second_down: float32 [2048, 640], P('group', 'replica'), may hold values from 16.384 to 262.144
- second_gains: float32 [3072], P(('group', 'replica')), may hold values from 16.384 to 262.144
Outputs:
- block_out: bfloat16 [8192, 640], P(('group', 'replica'))
- grad_in: bfloat16 [8192, 640], P(('group', 'replica'))
- grad_qkv: float32 [640, 1536], P('group', 'replica')
- grad_out: float32 [1024, 640], P('group', 'replica')
- grad_gate_up: float32 [640, 4096], P('group', 'replica')
- grad_down: float32 [2048, 640], P('group', 'replica')
- grad_gains: float32 [3072], P(('group', 'replica'))
- moment_qkv: float32 [640, 1536], P('group', 'replica')
- moment_out: float32 [1024, 640], P('group', 'replica')
- moment_gate_up: float32 [640, 4096], P('group', 'replica')
- moment_down: float32 [2048, 640], P('group', 'replica')
- moment_gains: float32 [3072], P(('group', 'replica'))
- new_qkv: float32 [640, 1536], P('group', 'replica')
- new_out: float32 [1024, 640], P('group', 'replica')
- new_gate_up: float32 [640, 4096], P('group', 'replica')
- new_down: float32 [2048, 640], P('group', 'replica')
- new_gains: float32 [3072], P(('group', 'replica'))
Inputs may be any that keep to these rules, and one draw needn't show every extreme that they name: `hidden_in`: entries are real-valued, of both signs, with row and column scales that differ. `cotangent`: entries are real-valued, of both signs. `segment_ids`: sequence numbers never fall along the tokens; every sequence other than the first and the last holds exactly 8192 tokens. Within a sequence the positions rise by one from token to token.
All inputs are finite; a program needn't handle non-finite values.
Results may differ from a plain program's by a relative error of at most 0.018.
Values may be sent and summed in bfloat16 or wider, within the bound.
A program may use at most 128 MiB of HBM per device.

v0:
```python
import jax
import jax.numpy as jnp
from jax import lax
from jax.sharding import PartitionSpec as P

D = 640
H = 4
HD = 256
FF = 2048
WINDOW = 512
STEP = 10


norm_epsilon = 1e-06
rope_base = 10000.0
beta_one = 0.9
beta_two = 0.999
adam_epsilon = 1e-08
learn_rate = 0.05
weight_decay = 0.1
neg_fill = -1e30


def shifted(value, axis, by):
    peers = lax.axis_size(axis)
    pairs = [(i, i + by) for i in range(peers) if 0 <= i + by < peers]
    return lax.ppermute(value, axis, pairs)


def norm_apply(values, gain):
    scale = lax.rsqrt(jnp.mean(values * values, axis=-1, keepdims=True) + norm_epsilon)
    return values * scale * (1.0 + gain)


def rope_tables(positions, width):
    freqs = rope_base ** (-jnp.arange(0, width, 2).astype(jnp.float32) / width)
    angles = positions.astype(jnp.float32)[:, None] * freqs[None, :]
    return (jnp.cos(angles), jnp.sin(angles))


def rope_apply(values, cosine, sine):
    half = values.shape[-1] // 2
    first = values[..., :half]
    second = values[..., half:]
    return jnp.concatenate(
        [first * cosine - second * sine, second * cosine + first * sine], axis=-1
    )


def gelu_product(gate, up):
    return jax.nn.gelu(gate, approximate=True) * up


def outer_sum(left, right):
    return lax.dot_general(
        left, right, (((0,), (0,)), ((), ())), preferred_element_type=jnp.float32
    )


def back_dot(grad, weight):
    return lax.dot_general(
        grad, weight, (((1,), (1,)), ((), ())), preferred_element_type=jnp.float32
    )


def adam_step(grad, first, second, old, decay):
    first_new = beta_one * first + (1.0 - beta_one) * grad
    second_new = beta_two * second + (1.0 - beta_two) * grad * grad
    first_hat = first_new / (1.0 - beta_one**STEP)
    second_hat = second_new / (1.0 - beta_two**STEP)
    new = old - learn_rate * (first_hat / (jnp.sqrt(second_hat) + adam_epsilon) + decay * old)
    return (second_new, new)


def body(
    hidden_in,
    cotangent,
    segment_ids,
    positions,
    w_qkv,
    w_out,
    w_gate_up,
    w_down,
    norm_gains,
    first_qkv,
    first_out,
    first_gate_up,
    first_down,
    first_gains,
    second_qkv,
    second_out,
    second_gate_up,
    second_down,
    second_gains,
):
    tokens = hidden_in.shape[0]
    scaling = HD ** (-0.5)
    full_qkv, full_out, full_gate_up, full_down = (
        lax.all_gather(w_qkv, "group", axis=0, tiled=True),
        lax.all_gather(w_out, "group", axis=0, tiled=True),
        lax.all_gather(w_gate_up, "group", axis=0, tiled=True),
        lax.all_gather(w_down, "group", axis=0, tiled=True),
    )
    gain_attn_in = norm_gains[0:D]
    gain_attn_out = norm_gains[D : 2 * D]
    gain_ffn_in = norm_gains[2 * D : 3 * D]
    gain_ffn_out = norm_gains[3 * D : 4 * D]
    gain_query = norm_gains[4 * D : 4 * D + HD]
    gain_key = norm_gains[4 * D + HD : 4 * D + 2 * HD]
    cosine, sine = rope_tables(positions, HD)

    def query_key(query_raw, key_raw, gain_q, gain_k):
        query_rot = rope_apply(norm_apply(query_raw, gain_q), cosine[:, None, :], sine[:, None, :])
        key_rot = rope_apply(norm_apply(key_raw, gain_k), cosine, sine)
        return (query_rot, key_rot)

    inputs = hidden_in.astype(jnp.float32)
    attn_in = norm_apply(inputs, gain_attn_in).astype(jnp.bfloat16)
    qkv = jnp.dot(attn_in, full_qkv, preferred_element_type=jnp.float32)
    query_raw = qkv[:, : H * HD].reshape(tokens, H, HD)
    key_raw = qkv[:, H * HD : (H + 1) * HD]
    value_raw = qkv[:, (H + 1) * HD :]
    query_rot, key_rot = query_key(query_raw, key_raw, gain_query, gain_key)
    query_low = query_rot.astype(jnp.bfloat16)
    keyval = jnp.concatenate([key_rot.astype(jnp.bfloat16), value_raw.astype(jnp.bfloat16)], axis=1)
    own_ids = jnp.stack([segment_ids + 1, positions])
    reaches = -(-WINDOW // tokens)
    key_parts = [keyval]
    id_parts = [own_ids]
    for reach in range(1, reaches + 1):
        key_parts.insert(0, shifted(keyval, ("group", "replica"), reach))
        id_parts.insert(0, shifted(own_ids, ("group", "replica"), reach))
    key_all = jnp.concatenate(key_parts, axis=0)
    ids_all = jnp.concatenate(id_parts, axis=1)
    key_low = key_all[:, :HD]
    value_low = key_all[:, HD:]
    gap = positions[:, None] - ids_all[1][None, :]
    allowed = (ids_all[0][None, :] == (segment_ids + 1)[:, None]) & (gap >= 0) & (gap < WINDOW)

    def masked_scores():
        scores = (
            jnp.einsum("thd,kd->htk", query_low, key_low, preferred_element_type=jnp.float32)
            * scaling
        )
        return jnp.where(allowed[None], scores, neg_fill)

    masked = masked_scores()
    peak = jnp.max(masked, axis=-1, keepdims=True)
    expo = jnp.exp(masked - peak)
    total = jnp.sum(expo, axis=-1, keepdims=True)
    probs_low = (expo / total).astype(jnp.bfloat16)
    mixed = jnp.einsum("htk,kd->thd", probs_low, value_low, preferred_element_type=jnp.float32)
    mixed_low = mixed.reshape(tokens, H * HD).astype(jnp.bfloat16)
    projected = jnp.dot(mixed_low, full_out, preferred_element_type=jnp.float32)
    residual = inputs + norm_apply(projected, gain_attn_out)
    ffn_in = norm_apply(residual, gain_ffn_in).astype(jnp.bfloat16)
    gate_up = jnp.dot(ffn_in, full_gate_up, preferred_element_type=jnp.float32)
    activated = gelu_product(gate_up[:, :FF], gate_up[:, FF:]).astype(jnp.bfloat16)
    down = jnp.dot(activated, full_down, preferred_element_type=jnp.float32)
    block_out = (residual + norm_apply(down, gain_ffn_out)).astype(jnp.bfloat16)
    full_qkv, full_out, full_gate_up, full_down = (
        lax.all_gather(w_qkv, "group", axis=0, tiled=True),
        lax.all_gather(w_out, "group", axis=0, tiled=True),
        lax.all_gather(w_gate_up, "group", axis=0, tiled=True),
        lax.all_gather(w_down, "group", axis=0, tiled=True),
    )
    upstream = cotangent.astype(jnp.float32)
    unused, pull = jax.vjp(norm_apply, down, gain_ffn_out)
    d_down, grad_ffn_out = pull(upstream)
    d_down_low = d_down.astype(jnp.bfloat16)
    d_activated = back_dot(d_down_low, full_down)
    unused, pull = jax.vjp(gelu_product, gate_up[:, :FF], gate_up[:, FF:])
    d_gate, d_up = pull(d_activated)
    d_gate_up_low = jnp.concatenate([d_gate, d_up], axis=1).astype(jnp.bfloat16)
    d_ffn_in = back_dot(d_gate_up_low, full_gate_up)
    unused, pull = jax.vjp(norm_apply, residual, gain_ffn_in)
    d_residual_ffn, grad_ffn_in = pull(d_ffn_in)
    d_residual = upstream + d_residual_ffn
    unused, pull = jax.vjp(norm_apply, projected, gain_attn_out)
    d_projected, grad_attn_out = pull(d_residual)
    d_projected_low = d_projected.astype(jnp.bfloat16)
    d_mixed_low = back_dot(d_projected_low, full_out).astype(jnp.bfloat16).reshape(tokens, H, HD)
    probs_again = jnp.exp(masked_scores() - peak) / total
    d_probs = jnp.einsum("thd,kd->htk", d_mixed_low, value_low, preferred_element_type=jnp.float32)
    d_scores = probs_again * (d_probs - jnp.sum(d_probs * probs_again, axis=-1, keepdims=True))
    d_scores_low = d_scores.astype(jnp.bfloat16)
    d_query = (
        jnp.einsum("htk,kd->thd", d_scores_low, key_low, preferred_element_type=jnp.float32)
        * scaling
    )
    d_keys = (
        jnp.einsum("htk,thd->kd", d_scores_low, query_low, preferred_element_type=jnp.float32)
        * scaling
    )
    d_values = jnp.einsum("htk,thd->kd", probs_low, d_mixed_low, preferred_element_type=jnp.float32)
    key_grads = jnp.concatenate([d_keys, d_values], axis=1)
    own_grads = key_grads[reaches * tokens :]
    for reach in range(1, reaches + 1):
        piece = key_grads[(reaches - reach) * tokens : (reaches - reach + 1) * tokens]
        own_grads = own_grads + shifted(
            piece.astype(jnp.bfloat16), ("group", "replica"), -reach
        ).astype(piece.dtype)
    unused, pull = jax.vjp(query_key, query_raw, key_raw, gain_query, gain_key)
    d_query_raw, d_key_raw, grad_query, grad_key = pull((d_query, own_grads[:, :HD]))
    d_qkv_low = jnp.concatenate(
        [d_query_raw.reshape(tokens, H * HD), d_key_raw, own_grads[:, HD:]], axis=1
    ).astype(jnp.bfloat16)
    d_attn_in = back_dot(d_qkv_low, full_qkv)
    unused, pull = jax.vjp(norm_apply, inputs, gain_attn_in)
    d_inputs, grad_attn_in = pull(d_attn_in)
    grad_in = (d_residual + d_inputs).astype(jnp.bfloat16)
    groups = lax.axis_size("group")
    replicas = lax.axis_size("replica")
    gain_terms = jnp.concatenate(
        [grad_attn_in, grad_attn_out, grad_ffn_in, grad_ffn_out, grad_query, grad_key]
    )
    column = lax.axis_index("replica")
    gain_rows = gain_terms.reshape(groups, gain_terms.shape[0] // groups)
    terms = (
        outer_sum(attn_in, d_qkv_low),
        outer_sum(mixed_low, d_projected_low),
        outer_sum(ffn_in, d_gate_up_low),
        outer_sum(activated, d_down_low),
        gain_rows,
    )
    row_sums = (
        lax.psum_scatter(
            terms[0].astype(jnp.bfloat16), "group", scatter_dimension=0, tiled=True
        ).astype(jnp.float32),
        lax.psum_scatter(
            terms[1].astype(jnp.bfloat16), "group", scatter_dimension=0, tiled=True
        ).astype(jnp.float32),
        lax.psum_scatter(
            terms[2].astype(jnp.bfloat16), "group", scatter_dimension=0, tiled=True
        ).astype(jnp.float32),
        lax.psum_scatter(
            terms[3].astype(jnp.bfloat16), "group", scatter_dimension=0, tiled=True
        ).astype(jnp.float32),
        lax.psum_scatter(
            terms[4].astype(jnp.bfloat16), "group", scatter_dimension=0, tiled=True
        ).astype(jnp.float32),
    )
    totals = lax.psum((row_sums[0], row_sums[1], row_sums[2], row_sums[3], row_sums[4]), "replica")
    owned = tuple(
        (
            lax.dynamic_slice_in_dim(
                item, column * (item.shape[1] // replicas), item.shape[1] // replicas, 1
            )
            for item in totals
        )
    )

    def old_columns(weight):
        width = weight.shape[1] // replicas
        return lax.dynamic_slice_in_dim(weight, column * width, width, 1).astype(jnp.float32)

    moment_qkv, new_qkv = adam_step(
        owned[0], first_qkv, second_qkv, old_columns(w_qkv), weight_decay
    )
    moment_out, new_out = adam_step(
        owned[1], first_out, second_out, old_columns(w_out), weight_decay
    )
    moment_gate_up, new_gate_up = adam_step(
        owned[2], first_gate_up, second_gate_up, old_columns(w_gate_up), weight_decay
    )
    moment_down, new_down = adam_step(
        owned[3], first_down, second_down, old_columns(w_down), weight_decay
    )
    grad_gains = owned[4].reshape(-1)
    share = grad_gains.shape[0]
    owner = lax.axis_index("group") * replicas + column
    old_gains = lax.dynamic_slice_in_dim(norm_gains, owner * share, share, 0)
    moment_gains, new_gains = adam_step(grad_gains, first_gains, second_gains, old_gains, 0.0)
    return (
        block_out,
        grad_in,
        owned[0],
        owned[1],
        owned[2],
        owned[3],
        grad_gains,
        moment_qkv,
        moment_out,
        moment_gate_up,
        moment_down,
        moment_gains,
        new_qkv,
        new_out,
        new_gate_up,
        new_down,
        new_gains,
    )


def solution(mesh):
    in_specs = (
        P(("group", "replica"), None),
        P(("group", "replica"), None),
        P(("group", "replica")),
        P(("group", "replica")),
        P("group", None),
        P("group", None),
        P("group", None),
        P("group", None),
        P(),
        P("group", "replica"),
        P("group", "replica"),
        P("group", "replica"),
        P("group", "replica"),
        P(("group", "replica")),
        P("group", "replica"),
        P("group", "replica"),
        P("group", "replica"),
        P("group", "replica"),
        P(("group", "replica")),
    )
    out_specs = (
        P(("group", "replica"), None),
        P(("group", "replica"), None),
        P("group", "replica"),
        P("group", "replica"),
        P("group", "replica"),
        P("group", "replica"),
        P(("group", "replica")),
        P("group", "replica"),
        P("group", "replica"),
        P("group", "replica"),
        P("group", "replica"),
        P(("group", "replica")),
        P("group", "replica"),
        P("group", "replica"),
        P("group", "replica"),
        P("group", "replica"),
        P(("group", "replica")),
    )
    return jax.shard_map(body, mesh=mesh, in_specs=in_specs, out_specs=out_specs, check_vma=False)
```

profile of v0, /device:TPU:0, one launch (start us, length us, event | category | flops | bytes accessed | tf_op | source)
XLA Modules:
  0.0 640.7 jit_solution(4805517673961121682)
XLA Ops:
  11.9 4.4 collective-permute-start.2
  18.0 38.0 %all-gather.5.cloned.1.call-done = bf16[640,1536]{1,0:T(8,128)(2,1)} async-done(((bf16[160,1536]{1,0:T(8,128)(2,1)}), bf16[640,1536]{1,0:T(8,128)(2,1)}) %all-gather.5.cloned.1.call-update) | async-done | bytes 1966096 | tf_op jit(solution)/shard_map/all_gather | solution.py:99
  61.1 3.6 collective-permute-start
  68.3 3.0 collective-permute-done
  72.0 3.2 fusion.98
  75.2 2.5 convolution_convert_fusion.5
  77.8 11.3 %all-gather.7.cloned.1.call-done = bf16[1024,640]{1,0:T(8,128)(2,1)} async-done(((bf16[256,640]{1,0:T(8,128)(2,1)}), bf16[1024,640]{1,0:T(8,128)(2,1)}) %all-gather.7.cloned.1.call-update) | async-done | bytes 1310736 | tf_op jit(solution)/shard_map/all_gather | solution.py:100
  91.4 102.1 %all-gather.9.cloned.1.call-done = bf16[640,4096]{1,0:T(8,128)(2,1)} async-done(((bf16[160,4096]{1,0:T(8,128)(2,1)}), bf16[640,4096]{1,0:T(8,128)(2,1)}) %all-gather.9.cloned.1.call-update) | async-done | bytes 5242896 | tf_op jit(solution)/shard_map/all_gather | solution.py:101
  193.4 4.3 fusion.92
  200.5 47.5 %all-gather.11.cloned.1.call-done = bf16[2048,640]{1,0:T(8,128)(2,1)} async-done(((bf16[512,640]{1,0:T(8,128)(2,1)}), bf16[2048,640]{1,0:T(8,128)(2,1)}) %all-gather.11.cloned.1.call-update) | async-done | bytes 2621456 | tf_op jit(solution)/shard_map/all_gather | solution.py:102
  248.1 2.9 multiply_reduce_fusion.6
  252.9 2.5 fusion.11
  255.5 2.5 multiply_reduce_fusion.2
  261.4 4.3 fusion.1
  265.7 3.5 convolution_bitcast_fusion
  270.8 3.4 fusion.3
  294.0 2.5 convolution_convert_fusion.1
  298.0 4.0 convolution_convert_fusion
  304.7 2.9 fusion.31
  308.9 18.6 %all-reduce.4 = bf16[4,768]{1,0:T(4,128)(2,1)S(1)} all-reduce(bf16[4,768]{1,0:T(4,128)(2,1)S(1)} %convert_element_type.138), channel_id=6, replica_groups=mesh['group'=4,'replica'=8] {'group'}, use_global_device_ids=true, to_apply=%region_29.30.clone | all-reduce | flops 3072 | bytes 12288
  330.2 25.6 %reduce-scatter.5.cloned.1.call-done = bf16[160,1536]{1,0:T(8,128)(2,1)} async-done(((bf16[640,1536]{1,0:T(8,128)(2,1)}), bf16[160,1536]{1,0:T(8,128)(2,1)}) %reduce-scatter.5.cloned.1.call-update) | async-done | bytes 491536 | tf_op jit(solution)/shard_map/reduce_scatter | solution.py:227
  355.9 53.8 %reduce-scatter.11.cloned.1.call-done = bf16[512,640]{1,0:T(8,128)(2,1)} async-done(((bf16[2048,640]{1,0:T(8,128)(2,1)}), bf16[512,640]{1,0:T(8,128)(2,1)}) %reduce-scatter.11.cloned.1.call-update) | async-done | bytes 655376 | tf_op jit(solution)/shard_map/reduce_scatter | solution.py:236
  409.7 95.8 %reduce-scatter.9.cloned.1.call-done = bf16[160,4096]{1,0:T(8,128)(2,1)} async-done(((bf16[640,4096]{1,0:T(8,128)(2,1)}), bf16[160,4096]{1,0:T(8,128)(2,1)}) %reduce-scatter.9.cloned.1.call-update) | async-done | bytes 1310736 | tf_op jit(solution)/shard_map/reduce_scatter | solution.py:233
  505.5 115.8 %all-reduce.7 = (f32[160,1536]{1,0:T(8,128)}, f32[256,640]{1,0:T(8,128)S(1)}, f32[160,4096]{1,0:T(8,128)}, f32[512,640]{1,0:T(8,128)}, f32[1,768]{1,0:T(1,128)S(1)}) all-reduce(bf16[160,1536]{1,0:T(8,128)(2,1)} %reduce-scatter.5.cloned.1.call-done, ...), channel_id=1, replica_groups=mesh['group'=4,'replica'=8] {'replica'}, use_global_device_ids=true, to_apply=%region_16.17 | all-reduce | flops 1393408 | bytes 8361984 | tf_op jit(solution)/shard_map/psum | solution.py:243
  (271 shorter events, 67.3 us)
Async XLA Ops:
  7.2 48.7 %all-gather.5.cloned.1.call-start = ((), (), s32[]{:S(2)}) async-start(), calls=%async_computation.4 | async-start | bytes 2457600 | tf_op jit(solution)/shard_map/all_gather | solution.py:99
  8.0 81.1 %all-gather.7.cloned.1.call-start = ((), (), s32[]{:S(2)}) async-start(), calls=%async_computation.5 | async-start | bytes 1638400 | tf_op jit(solution)/shard_map/all_gather | solution.py:100
  8.7 184.7 %all-gather.9.cloned.1.call-start = ((), (), s32[]{:S(2)}) async-start(), calls=%async_computation.6 | async-start | bytes 6553600 | tf_op jit(solution)/shard_map/all_gather | solution.py:101
  9.5 238.6 %all-gather.11.cloned.1.call-start = ((), (), s32[]{:S(2)}) async-start(), calls=%async_computation.7 | async-start | bytes 3276800 | tf_op jit(solution)/shard_map/all_gather | solution.py:102
  9.5 7.2 %collective-permute-start.3 = (s32[2,256]{1,0:T(2,128)S(1)}, s32[2,256]{1,0:T(2,128)S(1)}, u32[]{:S(2)}, u32[]{:S(2)}) collective-permute-start(s32[2,256]{1,0:T(2,128)S(1)} %pad_add_fusion.2), channel_id=1, source_target_pairs={{0,1},{1,2},{2,3},{3,4},{4,5},{5,6},{6,7},{7,8},{8,9},{9,10},{10,1... | collective-permute-start | bytes 6152 | tf_op jit(solution)/shard_map/ppermute | solution.py:27
  11.9 5.7 collective-permute-start.2
  16.3 313.9 %reduce-scatter.7.cloned.1.call-start = ((), (), s32[]{:S(2)}) async-start(), calls=%async_computation.9 | async-start | bytes 1638400 | tf_op jit(solution)/shard_map/reduce_scatter | solution.py:230
  16.4 42.1 %copy-start.52 = (f32[256]{0:T(256)}, f32[256]{0:T(256)S(1)}, u32[]{:S(2)}) copy-start(f32[256]{0:T(256)S(1)} %get-tuple-element.156) | copy-start | bytes 3076
  16.5 51.4 %copy-start.54 = (f32[256]{0:T(256)}, f32[256]{0:T(256)S(1)}, u32[]{:S(2)}) copy-start(f32[256]{0:T(256)S(1)} %get-tuple-element.155) | copy-start | bytes 3076
  16.6 41.7 %copy-start.57 = (f32[256]{0:T(256)}, f32[256]{0:T(256)S(1)}, u32[]{:S(2)}) copy-start(f32[256]{0:T(256)S(1)} %fusion.77) | copy-start | bytes 3076
  16.7 42.0 %copy-start.68 = (f32[128]{0:T(128)}, f32[128]{0:T(128)S(1)}, u32[]{:S(2)}) copy-start(f32[128]{0:T(128)S(1)} %multiply_power_fusion) | copy-start | bytes 1540
  16.7 42.0 %copy-start.59 = (f32[256]{0:T(256)}, f32[256]{0:T(256)S(1)}, u32[]{:S(2)}) copy-start(f32[256]{0:T(256)S(1)} %convert_element_type.113) | copy-start | bytes 3076
  59.3 9.0 %collective-permute-start.1 = (bf16[256,512]{1,0:T(8,128)(2,1)S(1)}, bf16[256,512]{1,0:T(8,128)(2,1)S(1)}, u32[]{:S(2)}, u32[]{:S(2)}) collective-permute-start(bf16[256,512]{1,0:T(8,128)(2,1)S(1)} %pad_maximum_fusion.10), channel_id=1, source_target_pairs={{0,1},{1,2},{2,3},{3,4},{4,5},{5,6},{6,7},{7,8},{8,9},{9,10},{10,1... | collective-permute-start | bytes 786440 | tf_op jit(solution)/shard_map/ppermute | solution.py:27
  61.1 10.2 %collective-permute-start = (bf16[256,512]{1,0:T(8,128)(2,1)S(1)}, bf16[256,512]{1,0:T(8,128)(2,1)S(1)}, u32[]{:S(2)}, u32[]{:S(2)}) collective-permute-start(bf16[256,512]{1,0:T(8,128)(2,1)S(1)} %pad_maximum_fusion.10), channel_id=1, source_target_pairs={{0,2},{1,3},{2,4},{3,5},{4,6},{5,7},{6,8},{7,9},{8,10},{9,11},{10,... | collective-permute-start | bytes 786440 | tf_op jit(solution)/shard_map/ppermute | solution.py:27
  77.8 13.3 %copy-start.17 = (bf16[256,4,256]{2,0,1:T(8,128)(2,1)}, bf16[256,4,256]{2,0,1:T(8,128)(2,1)S(1)}, u32[]{:S(2)}) copy-start(bf16[256,4,256]{2,0,1:T(8,128)(2,1)S(1)} %convolution_convert_fusion.5) | copy-start | bytes 1572868
  200.5 50.5 %copy-start.8 = (bf16[256,2048]{1,0:T(8,128)(2,1)}, bf16[256,2048]{1,0:T(8,128)(2,1)S(1)}, u32[]{:S(2)}) copy-start(bf16[256,2048]{1,0:T(8,128)(2,1)S(1)} %multiply_convert_fusion.1) | copy-start | bytes 3145732
  277.1 10.2 %collective-permute-start.5 = (bf16[256,512]{1,0:T(8,128)(2,1)}, bf16[256,512]{1,0:T(8,128)(2,1)}, u32[]{:S(2)}, u32[]{:S(2)}) collective-permute-start(bf16[256,512]{1,0:T(8,128)(2,1)} %get-tuple-element.144), channel_id=1, source_target_pairs={{2,0},{3,1},{4,2},{5,3},{6,4},{7,5},{8,6},{9,7},{10,8},{11,9},{12,... | collective-permute-start | bytes 786440 | tf_op jit(solution)/shard_map/ppermute | solution.py:27
  278.4 8.9 %collective-permute-start.4 = (bf16[256,512]{1,0:T(8,128)(2,1)}, bf16[256,512]{1,0:T(8,128)(2,1)}, u32[]{:S(2)}, u32[]{:S(2)}) collective-permute-start(bf16[256,512]{1,0:T(8,128)(2,1)} %get-tuple-element.143), channel_id=1, source_target_pairs={{1,0},{2,1},{3,2},{4,3},{5,4},{6,5},{7,6},{8,7},{9,8},{10,9},{11,1... | collective-permute-start | bytes 786440 | tf_op jit(solution)/shard_map/ppermute | solution.py:27
  279.8 76.0 %reduce-scatter.5.cloned.1.call-start = ((), (), s32[]{:S(2)}) async-start(), calls=%async_computation.8 | async-start | bytes 2457600 | tf_op jit(solution)/shard_map/reduce_scatter | solution.py:227
  293.9 115.8 %reduce-scatter.11.cloned.1.call-start = ((), (), s32[]{:S(2)}) async-start(), calls=%async_computation.11 | async-start | bytes 3276800 | tf_op jit(solution)/shard_map/reduce_scatter | solution.py:236
  296.5 209.0 %reduce-scatter.9.cloned.1.call-start = ((), (), s32[]{:S(2)}) async-start(), calls=%async_computation.10 | async-start | bytes 6553600 | tf_op jit(solution)/shard_map/reduce_scatter | solution.py:233
  304.7 23.5 %copy-start.62 = (f32[256]{0:T(256)S(1)}, f32[256]{0:T(256)}, u32[]{:S(2)}) copy-start(f32[256]{0:T(256)} %copy-done.61) | copy-start | bytes 3076
  304.7 23.5 %copy-start.4 = (f32[256,640]{1,0:T(8,128)S(1)}, f32[256,640]{1,0:T(8,128)}, u32[]{:S(2)}) copy-start(f32[256,640]{1,0:T(8,128)} %copy-done.3) | copy-start | bytes 1966084
  330.2 292.9 %copy-start.34 = (f32[512,80]{1,0:T(8,128)S(1)}, f32[512,80]{1,0:T(8,128)}, u32[]{:S(2)}) copy-start(f32[512,80]{1,0:T(8,128)} %copy.173) | copy-start | bytes 491524
  (67 other events, 251.6 us)
Sparse Core Ops, SparseCore 0:
  9.6 46.2 all-gather.4
  57.5 31.5 all-gather.6
  90.6 102.7 all-gather.8
  194.9 53.1 all-gather.10
  280.0 33.8 reduce-scatter.6
  316.0 39.8 reduce-scatter.4
  358.2 51.4 reduce-scatter.10
  412.0 93.4 reduce-scatter.8
where the time goes:
time: 642 us; the launch traced here: 641 us
  waiting for transfers between devices  382 us (60%)
  blocking collectives  134 us (21%)
  matrix products  43.7 us (7%)
  other arithmetic  30.5 us (5%)
  local copies, waits for them, and re-layouts  19.6 us (3%)
  between operations  15.4 us (2%)
  starting transfers between devices  15.3 us (2%)
    psum x1, blocking collectives, body(): lax.psum((row_sums[0], row_sums[1], row_sums[2], row_sums[3], row_sums[4]...  116 us
    all_gather x1, waiting for transfers between devices, body(): lax.all_gather(w_gate_up, 'group', axis=0, tiled=True)  102 us
    reduce_scatter x1, waiting for transfers between devices, body(): lax.psum_scatter(terms[2].astype(jnp.bfloat16), 'group', scatter_dimensio...  95.8 us
    reduce_scatter x1, waiting for transfers between devices, body(): lax.psum_scatter(terms[3].astype(jnp.bfloat16), 'group', scatter_dimensio...  53.8 us
    all_gather x1, waiting for transfers between devices, body(): lax.all_gather(w_down, 'group', axis=0, tiled=True)  47.5 us
    all_gather x1, waiting for transfers between devices, body(): lax.all_gather(w_qkv, 'group', axis=0, tiled=True)  38 us
    reduce_scatter x1, waiting for transfers between devices, body(): lax.psum_scatter(terms[0].astype(jnp.bfloat16), 'group', scatter_dimensio...  25.6 us
    unnamed x1, blocking collectives  18.6 us
  transfers between devices with their start and end apart: 14, of which 10 were waited for; matrix products, arithmetic and copies ran while one was open for 8% of the time, Pallas kernels for 0%

commit v1 on v0

--- a/solution.py
+++ b/solution.py
@@ -1,7 +1,13 @@
+import functools
+
 import jax
 import jax.numpy as jnp
 from jax import lax
+from jax.experimental import pallas as pl
+from jax.experimental.pallas import tpu as pltpu
 from jax.sharding import PartitionSpec as P
+
+MESH = pl.DeviceIdType.MESH
 
 D = 640
 H = 4
@@ -70,6 +76,365 @@
     second_hat = second_new / (1.0 - beta_two**STEP)
     new = old - learn_rate * (first_hat / (jnp.sqrt(second_hat) + adam_epsilon) + decay * old)
     return (second_new, new)
+
+
+def places():
+    g = lax.axis_index("group")
+    r = lax.axis_index("replica")
+    core = lax.rem(r, 2)
+    x = lax.rem(r // 2, 2)
+    y = r // 4
+    mate = r + 1 - 2 * core
+    over_x = 2 - 4 * x
+    over_y = 4 - 8 * y
+    step_one = over_x * (1 - core) + over_y * core
+    step_two = over_y * (1 - core) + over_x * core
+    return g, r, mate, step_one, step_two
+
+
+def meet(g, r, mate, one, two, groups):
+    barrier = pltpu.get_barrier_semaphore()
+    for to in (mate, one, two):
+        pl.semaphore_signal(barrier, inc=1, device_id=(g, to), device_id_type=MESH)
+    for far in range(1, groups):
+        to = lax.rem(g + far, groups)
+        pl.semaphore_signal(barrier, inc=1, device_id=(to, r), device_id_type=MESH)
+    pl.semaphore_wait(barrier, 2 + groups)
+
+
+def gather_kernel(groups, replicas, *refs):
+    shards, fulls = refs[:4], refs[4:8]
+    local_sem, a_send, a_recv, b_send, b_recv = refs[8:]
+    g, r, mate, step_one, step_two = places()
+    one, two = r + step_one, r + step_two
+    diagonal = r + step_one + step_two
+    chips = replicas // 2
+
+    def view(ref, which, height, base, index):
+        width = ref.shape[1]
+        if which == 0:
+            rows = height // 2
+            part = width // chips
+            return ref.at[
+                pl.ds(pl.multiple_of(base + lax.rem(index, 2) * rows, 16), rows),
+                pl.ds(pl.multiple_of((index // 2) * part, 128), part),
+            ]
+        if which == 2:
+            part = width // replicas
+            return ref.at[
+                pl.ds(pl.multiple_of(base, 16), height),
+                pl.ds(pl.multiple_of(index * part, 128), part),
+            ]
+        rows = height // replicas
+        return ref.at[pl.ds(pl.multiple_of(base + index * rows, 16), rows), :]
+
+    def place(which, group, index):
+        height = shards[which].shape[0]
+        return view(fulls[which], which, height, group * height, index)
+
+    def send(src, dst, send_sem, recv_sem, to):
+        return pltpu.make_async_remote_copy(
+            src_ref=src, dst_ref=dst, send_sem=send_sem, recv_sem=recv_sem,
+            device_id=to, device_id_type=MESH,
+        )
+
+    meet(g, r, mate, one, two, groups)
+    started = []
+    items = [(which, far) for which in range(4) for far in range(1, groups)]
+    for which, far in items:
+        shard = shards[which]
+        copy = send(
+            view(shard, which, shard.shape[0], 0, r),
+            place(which, g, r),
+            a_send.at[far - 1, which],
+            a_recv.at[far - 1, which],
+            (lax.rem(g + far, groups), r),
+        )
+        copy.start()
+        started.append(copy)
+    own = []
+    for which in range(4):
+        height = shards[which].shape[0]
+        copy = pltpu.make_async_copy(
+            shards[which],
+            fulls[which].at[pl.ds(pl.multiple_of(g * height, 16), height), :],
+            local_sem.at[which],
+        )
+        copy.start()
+        own.append(copy)
+
+    def push(item, slot, index, to):
+        which, far = items[item]
+        part = place(which, lax.rem(g + groups - far, groups), index)
+        copy = send(part, part, b_send.at[item, slot], b_recv.at[item, slot], (g, to))
+        copy.start()
+        started.append(copy)
+
+    def arrived(item, slot, index):
+        which, far = items[item]
+        part = place(which, lax.rem(g + groups - far, groups), index)
+        send(part, part, b_send.at[item, slot], b_recv.at[item, slot], (g, mate)).wait_recv()
+
+    for turn in range(len(items) + 2):
+        if turn < len(items):
+            which, far = items[turn]
+            part = place(which, lax.rem(g + groups - far, groups), r)
+            send(
+                part, part, a_send.at[far - 1, which], a_recv.at[far - 1, which], (g, mate)
+            ).wait_recv()
+            push(turn, 0, r, one)
+            push(turn, 1, r, two)
+            push(turn, 3, r, mate)
+        item = turn - 1
+        if 0 <= item < len(items):
+            arrived(item, 0, one)
+            push(item, 2, one, two)
+            push(item, 4, one, mate)
+        item = turn - 2
+        if 0 <= item < len(items):
+            arrived(item, 1, two)
+            push(item, 5, two, mate)
+            arrived(item, 2, diagonal)
+            push(item, 6, diagonal, mate)
+    for item in range(len(items)):
+        arrived(item, 3, mate)
+        arrived(item, 4, mate + step_two)
+        arrived(item, 5, mate + step_one)
+        arrived(item, 6, mate + step_one + step_two)
+    for copy in own:
+        copy.wait()
+    for copy in started:
+        copy.wait_send()
+
+
+def gather_weights(groups, replicas, *shards):
+    items = 4 * (groups - 1)
+    dma = pltpu.SemaphoreType.DMA
+    return pl.pallas_call(
+        functools.partial(gather_kernel, groups, replicas),
+        out_shape=[
+            jax.ShapeDtypeStruct((groups * s.shape[0], s.shape[1]), s.dtype) for s in shards
+        ],
+        in_specs=[pl.BlockSpec(memory_space=pl.ANY)] * 4,
+        out_specs=[pl.BlockSpec(memory_space=pl.ANY)] * 4,
+        scratch_shapes=[
+            dma((4,)),
+            dma((groups - 1, 4)),
+            dma((groups - 1, 4)),
+            dma((items, 7)),
+            dma((items, 7)),
+        ],
+        compiler_params=pltpu.CompilerParams(collective_id=1, has_side_effects=True),
+        cost_estimate=pl.CostEstimate(flops=0, bytes_accessed=25000000, transcendentals=0),
+        name="gather_weights",
+    )(*shards)
+
+
+lanes = 128
+
+
+def sum_kernel(groups, replicas, dims, *refs):
+    (at, dqkv, bt, dgu, dzt, o, dmt, f, gains) = refs[:9]
+    out_q, out_g, out_o, out_d, out_n = refs[9:14]
+    to_mate, kept, from_mate, from_one, from_two, from_far = refs[14:20]
+    c_send, c_recv, x_send, x_recv, y_send, y_recv, z_send, z_recv = refs[20:]
+    rows_in, q_wide, g_wide, thin, o_wide, d_wide, rows = dims
+    g, r, mate, step_one, step_two = places()
+    one, two = r + step_one, r + step_two
+
+    def dot(left, right):
+        return jnp.dot(left, right, preferred_element_type=jnp.float32).astype(jnp.bfloat16)
+
+    def compute(dst, group, index):
+        top = pl.ds(pl.multiple_of(group * rows_in, 16), rows_in)
+        side = pl.ds(pl.multiple_of(index * thin, 16), thin)
+
+        def columns(width, place):
+            return pl.ds(pl.multiple_of(place * width, 128), width)
+
+        at_row = 0
+        for left, right, height, width in (
+            (at[top, :], dqkv[:, columns(q_wide, index)], rows_in, q_wide),
+            (bt[top, :], dgu[:, columns(g_wide, index)], rows_in, g_wide),
+            (dzt[side, :], o[:, columns(o_wide, group)], thin, o_wide),
+            (dmt[side, :], f[:, columns(d_wide, group)], thin, d_wide),
+        ):
+            block = dot(left, right)
+            for stripe in range(width // lanes):
+                dst[pl.ds(at_row, height), :] = block[:, stripe * lanes : (stripe + 1) * lanes]
+                at_row += height
+        dst[pl.ds(at_row, 16), :] = gains[index, group]
+
+    def send(src, dst, send_sem, recv_sem, to):
+        return pltpu.make_async_remote_copy(
+            src_ref=src, dst_ref=dst, send_sem=send_sem, recv_sem=recv_sem,
+            device_id=to, device_id_type=MESH,
+        )
+
+    def add(dst, src):
+        part = 208
+        def body(i, carry):
+            here = pl.ds(pl.multiple_of(i * part, 16), part)
+            dst[here, :] = (
+                dst[here, :].astype(jnp.float32) + src[here, :].astype(jnp.float32)
+            ).astype(jnp.bfloat16)
+            return carry
+        lax.fori_loop(0, rows // part, body, 0)
+
+    def flips(m):
+        return 1 - m // 2, lax.rem((m + 1) // 2, 2)
+
+    def target(stage):
+        return lax.rem(g + 1 + stage, groups)
+
+    def mate_copy(stage, m):
+        return send(
+            to_mate.at[stage, m], from_mate.at[stage, m], c_send.at[stage, m], c_recv.at[stage, m],
+            (g, mate),
+        )
+
+    def one_copy(stage, m):
+        return send(
+            kept.at[stage, m], from_one.at[stage, 1 - m], x_send.at[stage, 1 - m],
+            x_recv.at[stage, 1 - m], (g, one),
+        )
+
+    def two_copy(stage):
+        return send(
+            kept.at[stage, 2], from_two.at[stage], y_send.at[stage], y_recv.at[stage], (g, two)
+        )
+
+    def far_copy(stage):
+        return send(
+            kept.at[stage, 3], from_far.at[stage], z_send.at[stage], z_recv.at[stage],
+            (target(stage), r),
+        )
+
+    def make(stage):
+        def for_mate(m, carry):
+            first, second = flips(m)
+            compute(
+                to_mate.at[stage, m], target(stage), mate + first * step_two + second * step_one
+            )
+            mate_copy(stage, m).start()
+            return carry
+
+        def for_me(m, carry):
+            first, second = flips(m)
+            compute(kept.at[stage, m], target(stage), r + first * step_one + second * step_two)
+            return carry
+
+        lax.fori_loop(0, 4, for_mate, 0)
+        lax.fori_loop(0, 4, for_me, 0)
+
+    def pass_one(stage):
+        for m in (1, 0):
+            mate_copy(stage, m).wait_recv()
+            add(kept.at[stage, m], from_mate.at[stage, m])
+            one_copy(stage, m).start()
+        for m in (2, 3):
+            mate_copy(stage, m).wait_recv()
+            add(kept.at[stage, m], from_mate.at[stage, m])
+
+    def pass_two(stage):
+        one_copy(stage, 1).wait_recv()
+        add(kept.at[stage, 2], from_one.at[stage, 0])
+        two_copy(stage).start()
+        one_copy(stage, 0).wait_recv()
+        add(kept.at[stage, 3], from_one.at[stage, 1])
+
+    def pass_far(stage):
+        two_copy(stage).wait_recv()
+        add(kept.at[stage, 3], from_two.at[stage])
+        if stage < groups - 1:
+            far_copy(stage).start()
+
+    meet(g, r, mate, one, two, groups)
+    for turn in range(groups + 3):
+        if turn < groups:
+            make(turn)
+        if 0 <= turn - 1 < groups:
+            pass_one(turn - 1)
+        if 0 <= turn - 2 < groups:
+            pass_two(turn - 2)
+        if 0 <= turn - 3 < groups:
+            pass_far(turn - 3)
+    for stage in range(groups - 1):
+        far_copy(stage).wait_recv()
+    at_row = 0
+    for out, height, width in (
+        (out_q, rows_in, q_wide),
+        (out_g, rows_in, g_wide),
+        (out_o, thin, o_wide),
+        (out_d, thin, d_wide),
+        (out_n, 16, lanes),
+    ):
+        for stripe in range(width // lanes):
+            here = pl.ds(at_row, height)
+            total = kept[groups - 1, 3, here, :].astype(jnp.float32)
+            for stage in range(groups - 1):
+                total = total + from_far[stage, here, :].astype(jnp.float32)
+            out[:, stripe * lanes : (stripe + 1) * lanes] = total
+            at_row += height
+    for stage in range(groups):
+        for m in range(4):
+            mate_copy(stage, m).wait_send()
+        for m in range(2):
+            one_copy(stage, m).wait_send()
+        two_copy(stage).wait_send()
+        if stage < groups - 1:
+            far_copy(stage).wait_send()
+
+
+def sum_gradients(groups, replicas, attn_in, d_qkv, ffn_in, d_gate_up, d_proj, mixed, d_down, act, gain_terms):
+    tokens = attn_in.shape[0]
+    rows_in = D // groups
+    thin = D // replicas
+    q_part = d_qkv.shape[1] // replicas
+    q_wide = -(-q_part // lanes) * lanes
+    g_wide = d_gate_up.shape[1] // replicas
+    o_wide = mixed.shape[1] // groups
+    d_wide = act.shape[1] // groups
+    d_qkv = jnp.pad(d_qkv.reshape(tokens, replicas, q_part), ((0, 0), (0, 0), (0, q_wide - q_part)))
+    d_qkv = d_qkv.reshape(tokens, replicas * q_wide)
+    share = gain_terms.shape[0] // (groups * replicas)
+    gains = gain_terms.reshape(groups, replicas, 1, share).transpose(1, 0, 2, 3)
+    gains = jnp.pad(gains, ((0, 0), (0, 0), (0, 15), (0, lanes - share))).astype(jnp.bfloat16)
+    rows = (rows_in * (q_wide + g_wide) + thin * (o_wide + d_wide)) // lanes + 16
+    dims = (rows_in, q_wide, g_wide, thin, o_wide, d_wide, rows)
+    dma = pltpu.SemaphoreType.DMA
+    vmem = pl.BlockSpec(memory_space=pltpu.VMEM)
+    f32 = jnp.float32
+    got = pl.pallas_call(
+        functools.partial(sum_kernel, groups, replicas, dims),
+        out_shape=[
+            jax.ShapeDtypeStruct((rows_in, q_wide), f32),
+            jax.ShapeDtypeStruct((rows_in, g_wide), f32),
+            jax.ShapeDtypeStruct((thin, o_wide), f32),
+            jax.ShapeDtypeStruct((thin, d_wide), f32),
+            jax.ShapeDtypeStruct((16, lanes), f32),
+        ],
+        in_specs=[vmem] * 9,
+        out_specs=[vmem] * 5,
+        scratch_shapes=[
+            pltpu.VMEM((groups, 4, rows, lanes), jnp.bfloat16),
+            pltpu.VMEM((groups, 4, rows, lanes), jnp.bfloat16),
+            pltpu.VMEM((groups, 4, rows, lanes), jnp.bfloat16),
+            pltpu.VMEM((groups, 2, rows, lanes), jnp.bfloat16),
+            pltpu.VMEM((groups, rows, lanes), jnp.bfloat16),
+            pltpu.VMEM((groups - 1, rows, lanes), jnp.bfloat16),
+            dma((groups, 4)), dma((groups, 4)),
+            dma((groups, 2)), dma((groups, 2)),
+            dma((groups,)), dma((groups,)),
+            dma((groups - 1,)), dma((groups - 1,)),
+        ],
+        compiler_params=pltpu.CompilerParams(
+            collective_id=2, has_side_effects=True, vmem_limit_bytes=48 * 1024 * 1024
+        ),
+        cost_estimate=pl.CostEstimate(flops=3000000000, bytes_accessed=12000000, transcendentals=0),
+        name="sum_gradients",
+    )(attn_in.T, d_qkv, ffn_in.T, d_gate_up, d_proj.T, mixed, d_down.T, act, gains)
+    return (got[0][:, :q_part], got[2].T, got[1], got[3].T, got[4][0, :share])
 
 
 def body(
@@ -95,12 +460,20 @@
 ):
     tokens = hidden_in.shape[0]
     scaling = HD ** (-0.5)
-    full_qkv, full_out, full_gate_up, full_down = (
-        lax.all_gather(w_qkv, "group", axis=0, tiled=True),
-        lax.all_gather(w_out, "group", axis=0, tiled=True),
-        lax.all_gather(w_gate_up, "group", axis=0, tiled=True),
-        lax.all_gather(w_down, "group", axis=0, tiled=True),
-    )
+    groups = lax.axis_size("group")
+    replicas = lax.axis_size("replica")
+    direct = (groups, replicas) == (4, 8)
+    if direct:
+        full_qkv, full_out, full_gate_up, full_down = gather_weights(
+            groups, replicas, w_qkv, w_out, w_gate_up, w_down
+        )
+    else:
+        full_qkv, full_out, full_gate_up, full_down = (
+            lax.all_gather(w_qkv, "group", axis=0, tiled=True),
+            lax.all_gather(w_out, "group", axis=0, tiled=True),
+            lax.all_gather(w_gate_up, "group", axis=0, tiled=True),
+            lax.all_gather(w_down, "group", axis=0, tiled=True),
+        )
     gain_attn_in = norm_gains[0:D]
     gain_attn_out = norm_gains[D : 2 * D]
     gain_ffn_in = norm_gains[2 * D : 3 * D]
@@ -158,12 +531,6 @@
     activated = gelu_product(gate_up[:, :FF], gate_up[:, FF:]).astype(jnp.bfloat16)
     down = jnp.dot(activated, full_down, preferred_element_type=jnp.float32)
     block_out = (residual + norm_apply(down, gain_ffn_out)).astype(jnp.bfloat16)
-    full_qkv, full_out, full_gate_up, full_down = (
-        lax.all_gather(w_qkv, "group", axis=0, tiled=True),
-        lax.all_gather(w_out, "group", axis=0, tiled=True),
-        lax.all_gather(w_gate_up, "group", axis=0, tiled=True),
-        lax.all_gather(w_down, "group", axis=0, tiled=True),
-    )
     upstream = cotangent.astype(jnp.float32)
     unused, pull = jax.vjp(norm_apply, down, gain_ffn_out)
     d_down, grad_ffn_out = pull(upstream)
@@ -209,46 +576,51 @@
     unused, pull = jax.vjp(norm_apply, inputs, gain_attn_in)
     d_inputs, grad_attn_in = pull(d_attn_in)
     grad_in = (d_residual + d_inputs).astype(jnp.bfloat16)
-    groups = lax.axis_size("group")
-    replicas = lax.axis_size("replica")
     gain_terms = jnp.concatenate(
         [grad_attn_in, grad_attn_out, grad_ffn_in, grad_ffn_out, grad_query, grad_key]
     )
     column = lax.axis_index("replica")
-    gain_rows = gain_terms.reshape(groups, gain_terms.shape[0] // groups)
-    terms = (
-        outer_sum(attn_in, d_qkv_low),
-        outer_sum(mixed_low, d_projected_low),
-        outer_sum(ffn_in, d_gate_up_low),
-        outer_sum(activated, d_down_low),
-        gain_rows,
-    )
-    row_sums = (
-        lax.psum_scatter(
-            terms[0].astype(jnp.bfloat16), "group", scatter_dimension=0, tiled=True
-        ).astype(jnp.float32),
-        lax.psum_scatter(
-            terms[1].astype(jnp.bfloat16), "group", scatter_dimension=0, tiled=True
-        ).astype(jnp.float32),
-        lax.psum_scatter(
-            terms[2].astype(jnp.bfloat16), "group", scatter_dimension=0, tiled=True
-        ).astype(jnp.float32),
-        lax.psum_scatter(
-            terms[3].astype(jnp.bfloat16), "group", scatter_dimension=0, tiled=True
-        ).astype(jnp.float32),
-        lax.psum_scatter(
-            terms[4].astype(jnp.bfloat16), "group", scatter_dimension=0, tiled=True
-        ).astype(jnp.float32),
-    )
-    totals = lax.psum((row_sums[0], row_sums[1], row_sums[2], row_sums[3], row_sums[4]), "replica")
-    owned = tuple(
-        (
-            lax.dynamic_slice_in_dim(
-                item, column * (item.shape[1] // replicas), item.shape[1] // replicas, 1
+    if direct:
+        owned = sum_gradients(
+            groups, replicas, attn_in, d_qkv_low, ffn_in, d_gate_up_low, d_projected_low,
+            mixed_low, d_down_low, activated, gain_terms,
+        )
+    else:
+        gain_rows = gain_terms.reshape(groups, gain_terms.shape[0] // groups)
+        terms = (
+            outer_sum(attn_in, d_qkv_low),
+            outer_sum(mixed_low, d_projected_low),
+            outer_sum(ffn_in, d_gate_up_low),
+            outer_sum(activated, d_down_low),
+            gain_rows,
+        )
+        row_sums = (
+            lax.psum_scatter(
+                terms[0].astype(jnp.bfloat16), "group", scatter_dimension=0, tiled=True
+            ).astype(jnp.float32),
+            lax.psum_scatter(
+                terms[1].astype(jnp.bfloat16), "group", scatter_dimension=0, tiled=True
+            ).astype(jnp.float32),
+            lax.psum_scatter(
+                terms[2].astype(jnp.bfloat16), "group", scatter_dimension=0, tiled=True
+            ).astype(jnp.float32),
+            lax.psum_scatter(
+                terms[3].astype(jnp.bfloat16), "group", scatter_dimension=0, tiled=True
+            ).astype(jnp.float32),
+            lax.psum_scatter(
+                terms[4].astype(jnp.bfloat16), "group", scatter_dimension=0, tiled=True
+            ).astype(jnp.float32),
+        )
+        totals = lax.psum((row_sums[0], row_sums[1], row_sums[2], row_sums[3], row_sums[4]), "replica")
+        owned = tuple(
+            (
+                lax.dynamic_slice_in_dim(
+                    item, column * (item.shape[1] // replicas), item.shape[1] // replicas, 1
+                )
+                for item in totals
             )
-            for item in totals
-        )
-    )
+        )
+        owned = owned[:4] + (owned[4].reshape(-1),)
 
     def old_columns(weight):
         width = weight.shape[1] // replicas
@@ -266,7 +638,7 @@
     moment_down, new_down = adam_step(
         owned[3], first_down, second_down, old_columns(w_down), weight_decay
     )
-    grad_gains = owned[4].reshape(-1)
+    grad_gains = owned[4]
     share = grad_gains.shape[0]
     owner = lax.axis_index("group") * replicas + column
     old_gains = lax.dynamic_slice_in_dim(norm_gains, owner * share, share, 0)

time: 642 us -> 285 us (0.44)
  waiting for transfers between devices: 382 us -> 0.66 us
  Pallas kernels: 0 us -> 165 us
  blocking collectives: 134 us -> 0 us
  local copies, waits for them, and re-layouts: 19.6 us -> 34.9 us
  matrix products: 43.7 us -> 29.1 us
  between operations: 15.4 us -> 1.81 us
    all_gather x4 -> x0, waiting for transfers between devices: 199 us -> none  [the longest x1 102 us: body(): lax.all_gather(w_gate_up, 'group', axis=0, tiled=True)]
    reduce_scatter x4 -> x0, waiting for transfers between devices: 175 us -> none  [the longest x1 95.8 us: body(): lax.psum_scatter(terms[2].astype(jnp.bfloat16), 'group', scatter_dimensio...]
    pallas_call x0 -> x2, Pallas kernels: none -> 165 us  [the longest x1 92.5 us: gather_weights(): pl.pallas_call(functools.partial(gather_kernel, groups, replicas), out_sh...]
    psum x1 -> x0, blocking collectives: 116 us -> none  [body(): lax.psum((row_sums[0], row_sums[1], row_sums[2], row_sums[3], row_sums[4]...]
    unnamed x1 -> x0, blocking collectives: 18.6 us -> none
    dot_general x4 -> x0, matrix products: 10.3 us -> none  [outer_sum(): lax.dot_general(left, right, (((0,), (0,)), ((), ())), preferred_element_...]
    unnamed x170 -> x178, local copies, waits for them, and re-layouts: 13.7 us -> 17.5 us
  transfers between devices with their start and end apart: 14 -> 6, of which waited for: 10 -> 1; matrix products, arithmetic and copies ran while one was open for 8% -> 5% of each run, Pallas kernels for 0% -> 0%
where the time goes in v1:
time: 285 us; the launch traced here: 283 us
  Pallas kernels  165 us (58%)
  other arithmetic  36.9 us (13%)
  local copies, waits for them, and re-layouts  34.9 us (12%)
  matrix products  29.1 us (10%)
  starting transfers between devices  15.1 us (5%)
    pallas_call x1, Pallas kernels, gather_weights(): pl.pallas_call(functools.partial(gather_kernel, groups, replicas), out_sh...  92.5 us
    pallas_call x1, Pallas kernels, sum_gradients(): pl.pallas_call(functools.partial(sum_kernel, groups, replicas, dims), out...  72.2 us
    unnamed x178, local copies, waits for them, and re-layouts  17.5 us
    ppermute x6, starting transfers between devices, shifted(): return lax.ppermute(value, axis, pairs)  15.1 us
    dot_general x4, matrix products, back_dot(): lax.dot_general(grad, weight, (((1,), (1,)), ((), ())), preferred_element...  11 us
    sub x5, other arithmetic, adam_step(): old - learn_rate * (first_hat / (jnp.sqrt(second_hat) + adam_epsilon) + d...  6.61 us
    reduce_sum x4, other arithmetic, norm_apply(): return values * scale * (1.0 + gain)  5.99 us
  transfers between devices with their start and end apart: 6, of which 1 were waited for; matrix products, arithmetic and copies ran while one was open for 5% of the time, Pallas kernels for 0%

profile of v1, /device:TPU:0, one launch (start us, length us, event | category | flops | bytes accessed | tf_op | source)
XLA Modules:
  0.0 283.2 jit_solution(8543967921885832130)
XLA Ops:
  3.4 92.5 %gather_weights.1 = (bf16[640,1536]{1,0:T(8,128)(2,1)}, bf16[1024,640]{1,0:T(8,128)(2,1)}, bf16[640,4096]{1,0:T(8,128)(2,1)}, bf16[2048,640]{1,0:T(8,128)(2,1)}) custom-call(bf16[160,1536]{1,0:T(8,128)(2,1)} %refs_0_.1, bf16[256,640]{1,0:T(8,128)(2,1)} %refs_1_.1, bf16[160,4096]{1,0:T(8,128)(2,1)} %refs_2_.1, bf16[512,640]{1,0:T(8,128)(2,1)} %refs_3_.1), custom_call_target="tpu_custom_call" | custom-call | bytes 25000000 | tf_op jit(solution)/shard_map/gather_weights/pallas_call | solution.py:213
  95.9 2.4 fusion.67
  100.9 2.2 collective-permute-start.1
  103.0 3.9 %collective-permute-start = (bf16[256,512]{1,0:T(8,128)(2,1)}, bf16[256,512]{1,0:T(8,128)(2,1)}, u32[]{:S(2)}, u32[]{:S(2)}) collective-permute-start(bf16[256,512]{1,0:T(8,128)(2,1)} %pad_maximum_fusion.5), channel_id=1, source_target_pairs={{0,2},{1,3},{2,4},{3,5},{4,6},{5,7},{6,8},{7,9},{8,10},{9,11},{10,... | collective-permute-start | bytes 786440 | tf_op jit(solution)/shard_map/ppermute | solution.py:33
  107.5 3.7 %collective-permute-start.3 = (s32[2,256]{1,0:T(2,128)}, s32[2,256]{1,0:T(2,128)}, u32[]{:S(2)}, u32[]{:S(2)}) collective-permute-start(s32[2,256]{1,0:T(2,128)} %pad_add_fusion.2), channel_id=1, source_target_pairs={{0,1},{1,2},{2,3},{3,4},{4,5},{5,6},{6,7},{7,8},{8,9},{9,10},{10,1... | collective-permute-start | bytes 6152 | tf_op jit(solution)/shard_map/ppermute | solution.py:33
  111.2 2.8 collective-permute-start.2
  127.9 4.4 %fusion.84 = f32[256,4096]{1,0:T(8,128)S(1)} fusion(bf16[640,4096]{1,0:T(8,128)(2,1)} %get-tuple-element.28, f32[256,640]{0,1:T(8,128)S(1)} %get-tuple-element.148, f32[640]{0:T(1024)S(1)} %get-tuple-element.167, f32[256]{0:T(256)S(1)} %fusion.76), kind=kOutput, calls=%fused_computation.193 | convolution fusion | flops 1342668800 | bytes 10096128 | tf_op jit(solution)/shard_map/dot_general | solution.py:530
  135.6 1.9 multiply_reduce_fusion.6
  137.5 2.2 copy.192
  139.7 2.2 fusion.31
  141.9 2.2 fusion.32
  144.1 4.2 %fusion.11 = (bf16[256,2048]{1,0:T(8,128)(2,1)S(1)}, bf16[256,2048]{1,0:T(8,128)(2,1)S(1)}) fusion(f32[256,4096]{1,0:T(8,128)} %copy-done.2, bf16[256,640]{0,1:T(8,128)(2,1)S(1)} %get-tuple-element.158, bf16[2048,640]{1,0:T(8,128)(2,1)S(1)} %copy-done.79), kind=kOutput, calls=%fused_computation.17 | convolution fusion | flops 683671552 | bytes 9240576 | tf_op jit(solution)/shard_map/dot_general | solution.py:67
  148.4 2.2 multiply_reduce_fusion.2
  154.8 2.1 copy.243
  156.9 2.8 fusion.1
  167.0 1.9 copy.221
  175.7 2.1 copy.205
  177.8 3.2 %pad_maximum_fusion.refs_3_ = bf16[256,4096]{1,0:T(8,128)(2,1)} fusion(bf16[256,2048]{1,0:T(8,128)(2,1)} %copy-done.30, bf16[256,2048]{1,0:T(8,128)(2,1)} %copy-done.29), kind=kLoop, calls=%fused_computation.18 | loop fusion | flops 4194304 | bytes 4194304 | tf_op jit(solution)/shard_map/concatenate | solution.py:541
  188.0 3.1 %fusion.29 = (bf16[640]{0:T(1024)(128)(2,1)}, f32[256]{0:T(256)S(1)}, f32[256,640]{0,1:T(8,128)S(1)}) fusion(bf16[256,640]{0,1:T(8,128)(2,1)S(1)} %copy-done.7, f32[256]{0:T(256)S(1)} %copy-done.47, f32[640]{0:T(1024)S(1)} %get-tuple-element.169, bf16[640,1536]{1,0:T(8,128)(2,1)} %get-tuple-element.26, bf16[256,256]{0,1:T(8,128)(2,1)S(1)} %copy.213, ...), kind=kOutput, calls=%fused_computation.71 | convolution fusion | flops 506821760 | bytes 3741440 | tf_op jit(solution)/shard_map/dot_general | solution.py:67
  193.2 1.9 copy.222
  195.1 2.2 pad.25
  202.2 72.2 %sum_gradients.1 = (f32[160,256]{1,0:T(8,128)S(1)}, f32[160,512]{1,0:T(8,128)S(1)}, f32[80,256]{1,0:T(8,128)S(1)}, f32[80,512]{1,0:T(8,128)S(1)}, f32[16,128]{1,0:T(8,128)S(1)}) custom-call(bf16[640,256]{1,0:T(8,128)(2,1)S(1)} %copy-done.1, bf16[256,2048]{1,0:T(8,128)(2,1)S(1)} %copy.240.refs_1_, bf16[640,256]{1,0:T(8,128)(2,1)S(1)} %copy-done, ...), custom_call_target="tpu_custom_call" | custom-call | flops 3000000000 | bytes 12000000 | tf_op jit(solution)/shard_map/sum_gradients/pallas_call | solution.py:408
  275.3 2.0 convert_subtract_fusion
  278.1 1.8 convert_subtract_fusion.2
  (258 shorter events, 59.4 us)
Async XLA Ops:
  0.7 98.8 %copy-start.73 = (f32[128]{0:T(128)}, f32[128]{0:T(128)S(1)}, u32[]{:S(2)}) copy-start(f32[128]{0:T(128)S(1)} %multiply_power_fusion) | copy-start | bytes 1540
  3.2 123.9 %copy-start.6 = (bf16[256,640]{0,1:T(8,128)(2,1)}, bf16[256,640]{0,1:T(8,128)(2,1)S(1)}, u32[]{:S(2)}) copy-start(bf16[256,640]{0,1:T(8,128)(2,1)S(1)} %copy.185) | copy-start | bytes 983044
  3.4 95.0 %copy-start.61 = (f32[256]{0:T(256)}, f32[256]{0:T(256)S(1)}, u32[]{:S(2)}) copy-start(f32[256]{0:T(256)S(1)} %fusion.36) | copy-start | bytes 3076
  3.4 95.0 %copy-start.46 = (f32[256]{0:T(256)}, f32[256]{0:T(256)S(1)}, u32[]{:S(2)}) copy-start(f32[256]{0:T(256)S(1)} %fusion.73) | copy-start | bytes 3076
  95.9 11.0 %copy-start.75 = (s32[256]{0:T(256)S(1)}, s32[256]{0:T(256)}, u32[]{:S(2)}) copy-start(s32[256]{0:T(256)} %param.21) | copy-start | bytes 3076
  98.4 15.7 %copy-start.5 = (f32[256,1536]{1,0:T(8,128)}, f32[256,1536]{1,0:T(8,128)S(1)}, u32[]{:S(2)}) copy-start(f32[256,1536]{1,0:T(8,128)S(1)} %fusion.67) | copy-start | bytes 4718596
  98.5 15.6 %copy-start.63 = (f32[256]{0:T(256)}, f32[256]{0:T(256)S(1)}, u32[]{:S(2)}) copy-start(f32[256]{0:T(256)S(1)} %multiply_reduce_fusion.11) | copy-start | bytes 3076
  99.4 14.8 %copy-start.51 = (f32[256]{0:T(256)}, f32[256]{0:T(256)S(1)}, u32[]{:S(2)}) copy-start(f32[256]{0:T(256)S(1)} %get-tuple-element.186) | copy-start | bytes 3076
  99.4 15.3 %copy-start.49 = (f32[256]{0:T(256)}, f32[256]{0:T(256)S(1)}, u32[]{:S(2)}) copy-start(f32[256]{0:T(256)S(1)} %get-tuple-element.171) | copy-start | bytes 3076
  99.4 16.8 %copy-start.53 = (f32[256]{0:T(256)}, f32[256]{0:T(256)S(1)}, u32[]{:S(2)}) copy-start(f32[256]{0:T(256)S(1)} %get-tuple-element.170) | copy-start | bytes 3076
  100.1 16.4 %copy-start.21 = (f32[256,128]{1,0:T(8,128)}, f32[256,128]{1,0:T(8,128)S(1)}, u32[]{:S(2)}) copy-start(f32[256,128]{1,0:T(8,128)S(1)} %get-tuple-element.172) | copy-start | bytes 393220
  100.1 16.4 %copy-start.23 = (f32[256,128]{1,0:T(8,128)}, f32[256,128]{1,0:T(8,128)S(1)}, u32[]{:S(2)}) copy-start(f32[256,128]{1,0:T(8,128)S(1)} %get-tuple-element.173) | copy-start | bytes 393220
  100.9 19.6 %collective-permute-start.1 = (bf16[256,512]{1,0:T(8,128)(2,1)}, bf16[256,512]{1,0:T(8,128)(2,1)}, u32[]{:S(2)}, u32[]{:S(2)}) collective-permute-start(bf16[256,512]{1,0:T(8,128)(2,1)} %pad_maximum_fusion.5), channel_id=1, source_target_pairs={{0,1},{1,2},{2,3},{3,4},{4,5},{5,6},{6,7},{7,8},{8,9},{9,10},{10,1... | collective-permute-start | bytes 786440 | tf_op jit(solution)/shard_map/ppermute | solution.py:33
  103.0 17.4 %collective-permute-start = (bf16[256,512]{1,0:T(8,128)(2,1)}, bf16[256,512]{1,0:T(8,128)(2,1)}, u32[]{:S(2)}, u32[]{:S(2)}) collective-permute-start(bf16[256,512]{1,0:T(8,128)(2,1)} %pad_maximum_fusion.5), channel_id=1, source_target_pairs={{0,2},{1,3},{2,4},{3,5},{4,6},{5,7},{6,8},{7,9},{8,10},{9,11},{10,... | collective-permute-start | bytes 786440 | tf_op jit(solution)/shard_map/ppermute | solution.py:33
  107.5 11.9 %collective-permute-start.3 = (s32[2,256]{1,0:T(2,128)}, s32[2,256]{1,0:T(2,128)}, u32[]{:S(2)}, u32[]{:S(2)}) collective-permute-start(s32[2,256]{1,0:T(2,128)} %pad_add_fusion.2), channel_id=1, source_target_pairs={{0,1},{1,2},{2,3},{3,4},{4,5},{5,6},{6,7},{7,8},{8,9},{9,10},{10,1... | collective-permute-start | bytes 6152 | tf_op jit(solution)/shard_map/ppermute | solution.py:33
  111.2 8.2 %collective-permute-start.2 = (s32[2,256]{1,0:T(2,128)}, s32[2,256]{1,0:T(2,128)}, u32[]{:S(2)}, u32[]{:S(2)}) collective-permute-start(s32[2,256]{1,0:T(2,128)} %pad_add_fusion.2), channel_id=1, source_target_pairs={{0,2},{1,3},{2,4},{3,5},{4,6},{5,7},{6,8},{7,9},{8,10},{9,11},{10,... | collective-permute-start | bytes 6152 | tf_op jit(solution)/shard_map/ppermute | solution.py:33
  127.1 23.6 %copy-start.48 = (f32[256]{0:T(256)}, f32[256]{0:T(256)S(1)}, u32[]{:S(2)}) copy-start(f32[256]{0:T(256)S(1)} %fusion.75) | copy-start | bytes 3076
  171.3 10.4 %collective-permute-start.5 = (bf16[256,512]{1,0:T(8,128)(2,1)}, bf16[256,512]{1,0:T(8,128)(2,1)}, u32[]{:S(2)}, u32[]{:S(2)}) collective-permute-start(bf16[256,512]{1,0:T(8,128)(2,1)} %get-tuple-element.156), channel_id=1, source_target_pairs={{2,0},{3,1},{4,2},{5,3},{6,4},{7,5},{8,6},{9,7},{10,8},{11,9},{12,... | collective-permute-start | bytes 786440 | tf_op jit(solution)/shard_map/ppermute | solution.py:33
  172.6 9.1 %collective-permute-start.4 = (bf16[256,512]{1,0:T(8,128)(2,1)}, bf16[256,512]{1,0:T(8,128)(2,1)}, u32[]{:S(2)}, u32[]{:S(2)}) collective-permute-start(bf16[256,512]{1,0:T(8,128)(2,1)} %get-tuple-element.155), channel_id=1, source_target_pairs={{1,0},{2,1},{3,2},{4,3},{5,4},{6,5},{7,6},{8,7},{9,8},{10,9},{11,1... | collective-permute-start | bytes 786440 | tf_op jit(solution)/shard_map/ppermute | solution.py:33
  202.2 72.3 %copy-start.38 = (bf16[256,80]{0,1:T(8,128)(2,1)S(1)}, bf16[256,80]{0,1:T(8,128)(2,1)}, u32[]{:S(2)}) copy-start(bf16[256,80]{0,1:T(8,128)(2,1)} %copy.241) | copy-start | bytes 122884
  202.2 72.3 %copy-start.41 = (f32[256,80]{0,1:T(8,128)S(1)}, f32[256,80]{0,1:T(8,128)}, u32[]{:S(2)}) copy-start(f32[256,80]{0,1:T(8,128)} %param.29) | copy-start | bytes 245764
  202.2 72.4 %copy-start.42 = (f32[256,80]{0,1:T(8,128)S(1)}, f32[256,80]{0,1:T(8,128)}, u32[]{:S(2)}) copy-start(f32[256,80]{0,1:T(8,128)} %param.34) | copy-start | bytes 245764
  202.2 73.1 %copy-start.34 = (f32[160,512]{1,0:T(8,128)S(1)}, f32[160,512]{1,0:T(8,128)}, u32[]{:S(2)}) copy-start(f32[160,512]{1,0:T(8,128)} %param.30) | copy-start | bytes 983044
  202.2 73.1 %copy-start.35 = (f32[160,512]{1,0:T(8,128)S(1)}, f32[160,512]{1,0:T(8,128)}, u32[]{:S(2)}) copy-start(f32[160,512]{1,0:T(8,128)} %param.35) | copy-start | bytes 983044
  (64 other events, 227.0 us)

commit v2 on v1

--- a/solution.py
+++ b/solution.py
@@ -215,8 +215,8 @@
         out_shape=[
             jax.ShapeDtypeStruct((groups * s.shape[0], s.shape[1]), s.dtype) for s in shards
         ],
-        in_specs=[pl.BlockSpec(memory_space=pl.ANY)] * 4,
-        out_specs=[pl.BlockSpec(memory_space=pl.ANY)] * 4,
+        in_specs=[pl.BlockSpec(memory_space=pltpu.VMEM)] * 4,
+        out_specs=[pl.BlockSpec(memory_space=pltpu.VMEM)] * 4,
         scratch_shapes=[
             dma((4,)),
             dma((groups - 1, 4)),
@@ -224,7 +224,9 @@
             dma((items, 7)),
             dma((items, 7)),
         ],
-        compiler_params=pltpu.CompilerParams(collective_id=1, has_side_effects=True),
+        compiler_params=pltpu.CompilerParams(
+            collective_id=1, has_side_effects=True, vmem_limit_bytes=48 * 1024 * 1024
+        ),
         cost_estimate=pl.CostEstimate(flops=0, bytes_accessed=25000000, transcendentals=0),
         name="gather_weights",
     )(*shards)
@@ -386,8 +388,8 @@
             far_copy(stage).wait_send()
 
 
-def sum_gradients(groups, replicas, attn_in, d_qkv, ffn_in, d_gate_up, d_proj, mixed, d_down, act, gain_terms):
-    tokens = attn_in.shape[0]
+def sum_gradients(groups, replicas, attn_in_t, d_qkv, ffn_in_t, d_gate_up, d_proj_t, mixed, d_down_t, act, gain_terms):
+    tokens = d_qkv.shape[0]
     rows_in = D // groups
     thin = D // replicas
     q_part = d_qkv.shape[1] // replicas
@@ -433,8 +435,274 @@
         ),
         cost_estimate=pl.CostEstimate(flops=3000000000, bytes_accessed=12000000, transcendentals=0),
         name="sum_gradients",
-    )(attn_in.T, d_qkv, ffn_in.T, d_gate_up, d_proj.T, mixed, d_down.T, act, gains)
+    )(attn_in_t, d_qkv, ffn_in_t, d_gate_up, d_proj_t, mixed, d_down_t, act, gains)
     return (got[0][:, :q_part], got[2].T, got[1], got[3].T, got[4][0, :share])
+
+
+def low(value):
+    return value.astype(jnp.bfloat16)
+
+
+def matmul(left, right):
+    return jnp.dot(left, right, preferred_element_type=jnp.float32)
+
+
+def rotate_norm(values, gain, cosine, sine):
+    return rope_apply(norm_apply(values, gain), cosine, sine)
+
+
+def before_kernel(hidden, w_qkv, gain_in, gain_q, gain_k, cosine, sine, attn_in_t, raw, query, keyval):
+    attn_in = norm_apply(hidden[...].astype(jnp.float32), gain_in[...])
+    attn_in_t[...] = low(attn_in.T)
+    attn_in = low(attn_in)
+    cos, sin = cosine[...], sine[...]
+    for head in range(H + 2):
+        here = slice(head * HD, (head + 1) * HD)
+        part = matmul(attn_in, w_qkv[:, here])
+        raw[:, here] = part
+        if head < H:
+            query[:, here] = low(rotate_norm(part, gain_q[...], cos, sin))
+        elif head == H:
+            keyval[:, :HD] = low(rotate_norm(part, gain_k[...], cos, sin))
+        else:
+            keyval[:, HD:] = low(part)
+
+
+def middle_kernel(
+    hidden, cotangent, query, keys, values, own_ids, key_ids, w_out, w_gate_up, w_down,
+    gain_attn_out, gain_ffn_in, gain_ffn_out,
+    block_out, mixed, ffn_in_t, act, d_down_t, d_gate_up, d_proj_t, d_query, d_keyval, d_residual,
+    g_attn_out, g_ffn_in, g_ffn_out,
+    bias, probs, gate_up, d_mixed, total,
+):
+    tokens = hidden.shape[0]
+    span = keys.shape[0]
+    scaling = HD ** (-0.5)
+    row = lax.broadcasted_iota(jnp.int32, (tokens, span), 0) + (span - tokens)
+    gap = row - lax.broadcasted_iota(jnp.int32, (tokens, span), 1)
+    allowed = (own_ids[...] == key_ids[...]) & (gap >= 0) & (gap < WINDOW)
+    bias[...] = jnp.where(allowed, 0.0, neg_fill)
+
+    def head_columns(head):
+        return pl.ds(pl.multiple_of(head * HD, HD), HD)
+
+    def attend(head, carry):
+        here = head_columns(head)
+        scores = back_dot(query[:, here], keys[...]) * scaling + bias[...]
+        expo = jnp.exp(scores - jnp.max(scores, axis=-1, keepdims=True))
+        soft = expo * (1.0 / jnp.sum(expo, axis=-1, keepdims=True))
+        probs[head] = soft
+        mixed[:, here] = low(matmul(low(soft), values[...]))
+        return carry
+
+    lax.fori_loop(0, H, attend, 0)
+    projected = matmul(mixed[...], w_out[...])
+    residual = hidden[...].astype(jnp.float32) + norm_apply(projected, gain_attn_out[...])
+    ffn_in = norm_apply(residual, gain_ffn_in[...])
+    ffn_in_t[...] = low(ffn_in.T)
+    ffn_low = low(ffn_in)
+    part = 512
+
+    def columns(i, base):
+        return pl.ds(pl.multiple_of(base + i * part, part), part)
+
+    total[...] = jnp.zeros_like(total)
+
+    def forward(i, carry):
+        gate = matmul(ffn_low, w_gate_up[:, columns(i, 0)])
+        up = matmul(ffn_low, w_gate_up[:, columns(i, FF)])
+        gate_up[:, columns(i, 0)] = gate
+        gate_up[:, columns(i, FF)] = up
+        product = low(gelu_product(gate, up))
+        act[:, columns(i, 0)] = product
+        total[...] += matmul(product, w_down[columns(i, 0), :])
+        return carry
+
+    lax.fori_loop(0, FF // part, forward, 0)
+    upstream = cotangent[...].astype(jnp.float32)
+    normed, pull = jax.vjp(norm_apply, total[...], gain_ffn_out[...])
+    block_out[...] = low(residual + normed)
+    d_down, g_ffn_out[...] = pull(upstream)
+    d_down_t[...] = low(d_down.T)
+    d_down_low = low(d_down)
+    total[...] = jnp.zeros_like(total)
+
+    def backward(i, carry):
+        d_act = back_dot(d_down_low, w_down[columns(i, 0), :])
+        unused, pull = jax.vjp(gelu_product, gate_up[:, columns(i, 0)], gate_up[:, columns(i, FF)])
+        d_gate, d_up = pull(d_act)
+        d_gate, d_up = low(d_gate), low(d_up)
+        d_gate_up[:, columns(i, 0)] = d_gate
+        d_gate_up[:, columns(i, FF)] = d_up
+        total[...] += back_dot(d_gate, w_gate_up[:, columns(i, 0)]) + back_dot(
+            d_up, w_gate_up[:, columns(i, FF)]
+        )
+        return carry
+
+    lax.fori_loop(0, FF // part, backward, 0)
+    unused, pull = jax.vjp(norm_apply, residual, gain_ffn_in[...])
+    d_residual_ffn, g_ffn_in[...] = pull(total[...])
+    d_res = upstream + d_residual_ffn
+    d_residual[...] = d_res
+    unused, pull = jax.vjp(norm_apply, projected, gain_attn_out[...])
+    d_proj, g_attn_out[...] = pull(d_res)
+    d_proj_t[...] = low(d_proj.T)
+    d_mixed[...] = low(back_dot(low(d_proj), w_out[...]))
+    d_keyval[...] = jnp.zeros_like(d_keyval)
+
+    def attend_back(head, carry):
+        here = head_columns(head)
+        soft = probs[head]
+        d_out = d_mixed[:, here]
+        d_probs = back_dot(d_out, values[...])
+        d_scores = low(soft * (d_probs - jnp.sum(d_probs * soft, axis=-1, keepdims=True)))
+        d_query[:, here] = matmul(d_scores, keys[...]) * scaling
+        d_keyval[:, :HD] += outer_sum(d_scores, query[:, here]) * scaling
+        d_keyval[:, HD:] += outer_sum(low(soft), d_out)
+        return carry
+
+    lax.fori_loop(0, H, attend_back, 0)
+
+
+def after_kernel(
+    hidden, w_qkv, gain_in, gain_q, gain_k, cosine, sine, raw, d_query, d_own, d_residual,
+    d_qkv, grad_in, g_in, g_q, g_k,
+):
+    cos, sin = cosine[...], sine[...]
+    sums = None
+    for head in range(H + 1):
+        here = slice(head * HD, (head + 1) * HD)
+        gain = gain_q if head < H else gain_k
+        unused, pull = jax.vjp(lambda v, w: rotate_norm(v, w, cos, sin), raw[:, here], gain[...])
+        d_raw, d_gain = pull(d_query[:, here] if head < H else d_own[:, :HD])
+        d_qkv[:, here] = low(d_raw)
+        if head < H:
+            sums = d_gain if sums is None else sums + d_gain
+        else:
+            g_k[...] = d_gain
+    g_q[...] = sums
+    d_qkv[:, (H + 1) * HD :] = low(d_own[:, HD:])
+    d_attn_in = back_dot(d_qkv[...], w_qkv[...])
+    unused, pull = jax.vjp(norm_apply, hidden[...].astype(jnp.float32), gain_in[...])
+    d_inputs, g_in[...] = pull(d_attn_in)
+    grad_in[...] = low(d_residual[...] + d_inputs)
+
+
+def plain_call(kernel, name, flops, outs, scratch, *args):
+    vmem = pl.BlockSpec(memory_space=pltpu.VMEM)
+    return pl.pallas_call(
+        kernel,
+        out_shape=[jax.ShapeDtypeStruct(shape, kind) for shape, kind in outs],
+        in_specs=[vmem] * len(args),
+        out_specs=[vmem] * len(outs),
+        scratch_shapes=scratch,
+        compiler_params=pltpu.CompilerParams(vmem_limit_bytes=56 * 1024 * 1024),
+        cost_estimate=pl.CostEstimate(flops=flops, bytes_accessed=10000000, transcendentals=0),
+        name=name,
+    )(*args)
+
+
+def layer_grads(
+    hidden_in, cotangent, segment_ids, positions, full_qkv, full_out, full_gate_up, full_down, norm_gains
+):
+    tokens = hidden_in.shape[0]
+    f32, b16 = jnp.float32, jnp.bfloat16
+    gains = norm_gains[None, :]
+    gain_attn_in, gain_attn_out, gain_ffn_in, gain_ffn_out = (
+        gains[:, i * D : (i + 1) * D] for i in range(4)
+    )
+    gain_query = gains[:, 4 * D : 4 * D + HD]
+    gain_key = gains[:, 4 * D + HD : 4 * D + 2 * HD]
+    cosine, sine = rope_tables(positions, HD)
+    wide = (H + 2) * HD
+    attn_in_t, raw, query, keyval = plain_call(
+        before_kernel, "before_attention", 2 * tokens * D * wide,
+        [((D, tokens), b16), ((tokens, wide), f32), ((tokens, H * HD), b16), ((tokens, 2 * HD), b16)],
+        [], hidden_in, full_qkv, gain_attn_in, gain_query, gain_key, cosine, sine,
+    )
+    reaches = -(-WINDOW // tokens)
+    marks = jnp.broadcast_to((segment_ids + 1).astype(b16)[:, None], (tokens, lanes))
+    moved = jnp.concatenate([keyval, marks], axis=1)
+    parts = [moved]
+    for reach in range(1, reaches + 1):
+        parts.insert(0, shifted(moved, ("group", "replica"), reach))
+    span = (reaches + 1) * tokens
+    every = jnp.concatenate(parts, axis=0)
+    key_ids = every[:, 2 * HD].astype(jnp.int32)[None, :]
+    own_ids = (segment_ids + 1)[:, None]
+    gain_out = ((1, D), f32)
+    (
+        block_out, mixed, ffn_in_t, act, d_down_t, d_gate_up, d_proj_t, d_query, d_keyval, d_residual,
+        g_attn_out, g_ffn_in, g_ffn_out,
+    ) = plain_call(
+        middle_kernel, "attention_and_ffn", 8000000000,
+        [
+            ((tokens, D), b16), ((tokens, H * HD), b16), ((D, tokens), b16), ((tokens, FF), b16),
+            ((D, tokens), b16), ((tokens, 2 * FF), b16), ((D, tokens), b16), ((tokens, H * HD), f32),
+            ((span, 2 * HD), f32), ((tokens, D), f32), gain_out, gain_out, gain_out,
+        ],
+        [
+            pltpu.VMEM((tokens, span), f32), pltpu.VMEM((H, tokens, span), f32),
+            pltpu.VMEM((tokens, 2 * FF), f32), pltpu.VMEM((tokens, H * HD), b16),
+            pltpu.VMEM((tokens, D), f32),
+        ],
+        hidden_in, cotangent, query, every[:, :HD], every[:, HD : 2 * HD], own_ids, key_ids,
+        full_out, full_gate_up, full_down, gain_attn_out, gain_ffn_in, gain_ffn_out,
+    )
+    d_own = d_keyval[reaches * tokens :]
+    for reach in range(1, reaches + 1):
+        piece = d_keyval[(reaches - reach) * tokens : (reaches - reach + 1) * tokens]
+        d_own = d_own + shifted(piece.astype(b16), ("group", "replica"), -reach).astype(f32)
+    d_qkv, grad_in, g_in, g_q, g_k = plain_call(
+        after_kernel, "after_attention", 2 * tokens * D * wide,
+        [((tokens, wide), b16), ((tokens, D), b16), gain_out, ((1, HD), f32), ((1, HD), f32)],
+        [], hidden_in, full_qkv, gain_attn_in, gain_query, gain_key, cosine, sine, raw, d_query, d_own,
+        d_residual,
+    )
+    gain_terms = jnp.concatenate([g_in, g_attn_out, g_ffn_in, g_ffn_out, g_q, g_k], axis=1)[0]
+    return block_out, grad_in, (
+        attn_in_t, d_qkv, ffn_in_t, d_gate_up, d_proj_t, mixed, d_down_t, act, gain_terms
+    )
+
+
+def owned_sums(groups, replicas, terms):
+    attn_in_t, d_qkv, ffn_in_t, d_gate_up, d_proj_t, mixed, d_down_t, act, gain_terms = terms
+    column = lax.axis_index("replica")
+    gain_rows = gain_terms.reshape(groups, gain_terms.shape[0] // groups)
+    terms = (
+        matmul(attn_in_t, d_qkv),
+        outer_sum(mixed, d_proj_t.T),
+        matmul(ffn_in_t, d_gate_up),
+        outer_sum(act, d_down_t.T),
+        gain_rows,
+    )
+    row_sums = (
+        lax.psum_scatter(
+            terms[0].astype(jnp.bfloat16), "group", scatter_dimension=0, tiled=True
+        ).astype(jnp.float32),
+        lax.psum_scatter(
+            terms[1].astype(jnp.bfloat16), "group", scatter_dimension=0, tiled=True
+        ).astype(jnp.float32),
+        lax.psum_scatter(
+            terms[2].astype(jnp.bfloat16), "group", scatter_dimension=0, tiled=True
+        ).astype(jnp.float32),
+        lax.psum_scatter(
+            terms[3].astype(jnp.bfloat16), "group", scatter_dimension=0, tiled=True
+        ).astype(jnp.float32),
+        lax.psum_scatter(
+            terms[4].astype(jnp.bfloat16), "group", scatter_dimension=0, tiled=True
+        ).astype(jnp.float32),
+    )
+    totals = lax.psum((row_sums[0], row_sums[1], row_sums[2], row_sums[3], row_sums[4]), "replica")
+    owned = tuple(
+        (
+            lax.dynamic_slice_in_dim(
+                item, column * (item.shape[1] // replicas), item.shape[1] // replicas, 1
+            )
+            for item in totals
+        )
+    )
+    return owned[:4] + (owned[4].reshape(-1),)
 
 
 def body(
@@ -458,8 +726,6 @@
     second_down,
     second_gains,
 ):
-    tokens = hidden_in.shape[0]
-    scaling = HD ** (-0.5)
     groups = lax.axis_size("group")
     replicas = lax.axis_size("replica")
     direct = (groups, replicas) == (4, 8)
@@ -474,153 +740,14 @@
             lax.all_gather(w_gate_up, "group", axis=0, tiled=True),
             lax.all_gather(w_down, "group", axis=0, tiled=True),
         )
-    gain_attn_in = norm_gains[0:D]
-    gain_attn_out = norm_gains[D : 2 * D]
-    gain_ffn_in = norm_gains[2 * D : 3 * D]
-    gain_ffn_out = norm_gains[3 * D : 4 * D]
-    gain_query = norm_gains[4 * D : 4 * D + HD]
-    gain_key = norm_gains[4 * D + HD : 4 * D + 2 * HD]
-    cosine, sine = rope_tables(positions, HD)
-
-    def query_key(query_raw, key_raw, gain_q, gain_k):
-        query_rot = rope_apply(norm_apply(query_raw, gain_q), cosine[:, None, :], sine[:, None, :])
-        key_rot = rope_apply(norm_apply(key_raw, gain_k), cosine, sine)
-        return (query_rot, key_rot)
-
-    inputs = hidden_in.astype(jnp.float32)
-    attn_in = norm_apply(inputs, gain_attn_in).astype(jnp.bfloat16)
-    qkv = jnp.dot(attn_in, full_qkv, preferred_element_type=jnp.float32)
-    query_raw = qkv[:, : H * HD].reshape(tokens, H, HD)
-    key_raw = qkv[:, H * HD : (H + 1) * HD]
-    value_raw = qkv[:, (H + 1) * HD :]
-    query_rot, key_rot = query_key(query_raw, key_raw, gain_query, gain_key)
-    query_low = query_rot.astype(jnp.bfloat16)
-    keyval = jnp.concatenate([key_rot.astype(jnp.bfloat16), value_raw.astype(jnp.bfloat16)], axis=1)
-    own_ids = jnp.stack([segment_ids + 1, positions])
-    reaches = -(-WINDOW // tokens)
-    key_parts = [keyval]
-    id_parts = [own_ids]
-    for reach in range(1, reaches + 1):
-        key_parts.insert(0, shifted(keyval, ("group", "replica"), reach))
-        id_parts.insert(0, shifted(own_ids, ("group", "replica"), reach))
-    key_all = jnp.concatenate(key_parts, axis=0)
-    ids_all = jnp.concatenate(id_parts, axis=1)
-    key_low = key_all[:, :HD]
-    value_low = key_all[:, HD:]
-    gap = positions[:, None] - ids_all[1][None, :]
-    allowed = (ids_all[0][None, :] == (segment_ids + 1)[:, None]) & (gap >= 0) & (gap < WINDOW)
-
-    def masked_scores():
-        scores = (
-            jnp.einsum("thd,kd->htk", query_low, key_low, preferred_element_type=jnp.float32)
-            * scaling
-        )
-        return jnp.where(allowed[None], scores, neg_fill)
-
-    masked = masked_scores()
-    peak = jnp.max(masked, axis=-1, keepdims=True)
-    expo = jnp.exp(masked - peak)
-    total = jnp.sum(expo, axis=-1, keepdims=True)
-    probs_low = (expo / total).astype(jnp.bfloat16)
-    mixed = jnp.einsum("htk,kd->thd", probs_low, value_low, preferred_element_type=jnp.float32)
-    mixed_low = mixed.reshape(tokens, H * HD).astype(jnp.bfloat16)
-    projected = jnp.dot(mixed_low, full_out, preferred_element_type=jnp.float32)
-    residual = inputs + norm_apply(projected, gain_attn_out)
-    ffn_in = norm_apply(residual, gain_ffn_in).astype(jnp.bfloat16)
-    gate_up = jnp.dot(ffn_in, full_gate_up, preferred_element_type=jnp.float32)
-    activated = gelu_product(gate_up[:, :FF], gate_up[:, FF:]).astype(jnp.bfloat16)
-    down = jnp.dot(activated, full_down, preferred_element_type=jnp.float32)
-    block_out = (residual + norm_apply(down, gain_ffn_out)).astype(jnp.bfloat16)
-    upstream = cotangent.astype(jnp.float32)
-    unused, pull = jax.vjp(norm_apply, down, gain_ffn_out)
-    d_down, grad_ffn_out = pull(upstream)
-    d_down_low = d_down.astype(jnp.bfloat16)
-    d_activated = back_dot(d_down_low, full_down)
-    unused, pull = jax.vjp(gelu_product, gate_up[:, :FF], gate_up[:, FF:])
-    d_gate, d_up = pull(d_activated)
-    d_gate_up_low = jnp.concatenate([d_gate, d_up], axis=1).astype(jnp.bfloat16)
-    d_ffn_in = back_dot(d_gate_up_low, full_gate_up)
-    unused, pull = jax.vjp(norm_apply, residual, gain_ffn_in)
-    d_residual_ffn, grad_ffn_in = pull(d_ffn_in)
-    d_residual = upstream + d_residual_ffn
-    unused, pull = jax.vjp(norm_apply, projected, gain_attn_out)
-    d_projected, grad_attn_out = pull(d_residual)
-    d_projected_low = d_projected.astype(jnp.bfloat16)
-    d_mixed_low = back_dot(d_projected_low, full_out).astype(jnp.bfloat16).reshape(tokens, H, HD)
-    probs_again = jnp.exp(masked_scores() - peak) / total
-    d_probs = jnp.einsum("thd,kd->htk", d_mixed_low, value_low, preferred_element_type=jnp.float32)
-    d_scores = probs_again * (d_probs - jnp.sum(d_probs * probs_again, axis=-1, keepdims=True))
-    d_scores_low = d_scores.astype(jnp.bfloat16)
-    d_query = (
-        jnp.einsum("htk,kd->thd", d_scores_low, key_low, preferred_element_type=jnp.float32)
-        * scaling
-    )
-    d_keys = (
-        jnp.einsum("htk,thd->kd", d_scores_low, query_low, preferred_element_type=jnp.float32)
-        * scaling
-    )
-    d_values = jnp.einsum("htk,thd->kd", probs_low, d_mixed_low, preferred_element_type=jnp.float32)
-    key_grads = jnp.concatenate([d_keys, d_values], axis=1)
-    own_grads = key_grads[reaches * tokens :]
-    for reach in range(1, reaches + 1):
-        piece = key_grads[(reaches - reach) * tokens : (reaches - reach + 1) * tokens]
-        own_grads = own_grads + shifted(
-            piece.astype(jnp.bfloat16), ("group", "replica"), -reach
-        ).astype(piece.dtype)
-    unused, pull = jax.vjp(query_key, query_raw, key_raw, gain_query, gain_key)
-    d_query_raw, d_key_raw, grad_query, grad_key = pull((d_query, own_grads[:, :HD]))
-    d_qkv_low = jnp.concatenate(
-        [d_query_raw.reshape(tokens, H * HD), d_key_raw, own_grads[:, HD:]], axis=1
-    ).astype(jnp.bfloat16)
-    d_attn_in = back_dot(d_qkv_low, full_qkv)
-    unused, pull = jax.vjp(norm_apply, inputs, gain_attn_in)
-    d_inputs, grad_attn_in = pull(d_attn_in)
-    grad_in = (d_residual + d_inputs).astype(jnp.bfloat16)
-    gain_terms = jnp.concatenate(
-        [grad_attn_in, grad_attn_out, grad_ffn_in, grad_ffn_out, grad_query, grad_key]
-    )
+    block_out, grad_in, terms = layer_grads(
+        hidden_in, cotangent, segment_ids, positions, full_qkv, full_out, full_gate_up, full_down, norm_gains
+    )
+    if direct:
+        owned = sum_gradients(groups, replicas, *terms)
+    else:
+        owned = owned_sums(groups, replicas, terms)
     column = lax.axis_index("replica")
-    if direct:
-        owned = sum_gradients(
-            groups, replicas, attn_in, d_qkv_low, ffn_in, d_gate_up_low, d_projected_low,
-            mixed_low, d_down_low, activated, gain_terms,
-        )
-    else:
-        gain_rows = gain_terms.reshape(groups, gain_terms.shape[0] // groups)
-        terms = (
-            outer_sum(attn_in, d_qkv_low),
-            outer_sum(mixed_low, d_projected_low),
-            outer_sum(ffn_in, d_gate_up_low),
-            outer_sum(activated, d_down_low),
-            gain_rows,
-        )
-        row_sums = (
-            lax.psum_scatter(
-                terms[0].astype(jnp.bfloat16), "group", scatter_dimension=0, tiled=True
-            ).astype(jnp.float32),
-            lax.psum_scatter(
-                terms[1].astype(jnp.bfloat16), "group", scatter_dimension=0, tiled=True
-            ).astype(jnp.float32),
-            lax.psum_scatter(
-                terms[2].astype(jnp.bfloat16), "group", scatter_dimension=0, tiled=True
-            ).astype(jnp.float32),
-            lax.psum_scatter(
-                terms[3].astype(jnp.bfloat16), "group", scatter_dimension=0, tiled=True
-            ).astype(jnp.float32),
-            lax.psum_scatter(
-                terms[4].astype(jnp.bfloat16), "group", scatter_dimension=0, tiled=True
-            ).astype(jnp.float32),
-        )
-        totals = lax.psum((row_sums[0], row_sums[1], row_sums[2], row_sums[3], row_sums[4]), "replica")
-        owned = tuple(
-            (
-                lax.dynamic_slice_in_dim(
-                    item, column * (item.shape[1] // replicas), item.shape[1] // replicas, 1
-                )
-                for item in totals
-            )
-        )
-        owned = owned[:4] + (owned[4].reshape(-1),)
 
     def old_columns(weight):
         width = weight.shape[1] // replicas

time: 285 us -> 234 us (0.82)
  matrix products: 29.1 us -> 0 us
  other arithmetic: 36.9 us -> 17.2 us
  waiting for transfers between devices: 0.66 us -> 17.4 us
  local copies, waits for them, and re-layouts: 34.9 us -> 22.2 us
  starting transfers between devices: 15.1 us -> 7.37 us
    pallas_call x0 -> x3, Pallas kernels: none -> 34.1 us  [plain_call(): pl.pallas_call(kernel, out_shape=[jax.ShapeDtypeStruct(shape, kind) for s...]
    pallas_call x1, Pallas kernels: 92.5 us -> 59.1 us  [gather_weights(): pl.pallas_call(functools.partial(gather_kernel, groups, replicas), out_sh...]
    dot_general x14 -> x0, matrix products: 29.1 us -> none  [the longest x4 11 us: back_dot(): lax.dot_general(grad, weight, (((1,), (1,)), ((), ())), preferred_element...]
    ppermute x6 -> x4, waiting for transfers between devices: 0.66 us -> 17.4 us  [shifted(): return lax.ppermute(value, axis, pairs)]
    ppermute x6 -> x4, starting transfers between devices: 15.1 us -> 7.37 us  [shifted(): return lax.ppermute(value, axis, pairs)]
    reduce_sum x8 -> x0, other arithmetic: 6.76 us -> none  [the longest x4 5.99 us: norm_apply(): return values * scale * (1.0 + gain)]
    unnamed x178 -> x57, local copies, waits for them, and re-layouts: 17.5 us -> 11 us
    convert_element_type x5 -> x1, other arithmetic: 5.27 us -> 0.18 us  [layer_grads(): key_ids = every[:, 2 * HD].astype(jnp.int32)[None, :]]
  transfers between devices with their start and end apart: 6 -> 4, of which waited for: 1 -> 3; matrix products, arithmetic and copies ran while one was open for 5% -> 1% of each run, Pallas kernels for 0% -> 0%
where the time goes in v2:
time: 234 us; the launch traced here: 233 us
  Pallas kernels  167 us (71%)
  local copies, waits for them, and re-layouts  22.2 us (9%)
  waiting for transfers between devices  17.4 us (7%)
  other arithmetic  17.2 us (7%)
  starting transfers between devices  7.37 us (3%)
    pallas_call x1, Pallas kernels, sum_gradients(): pl.pallas_call(functools.partial(sum_kernel, groups, replicas, dims), out...  74.2 us
    pallas_call x1, Pallas kernels, gather_weights(): pl.pallas_call(functools.partial(gather_kernel, groups, replicas), out_sh...  59.1 us
    pallas_call x3, Pallas kernels, plain_call(): pl.pallas_call(kernel, out_shape=[jax.ShapeDtypeStruct(shape, kind) for s...  34.1 us
    ppermute x4, waiting for transfers between devices, shifted(): return lax.ppermute(value, axis, pairs)  17.4 us
    unnamed x57, local copies, waits for them, and re-layouts  11 us
    ppermute x4, starting transfers between devices, shifted(): return lax.ppermute(value, axis, pairs)  7.37 us
    sub x5, other arithmetic, adam_step(): old - learn_rate * (first_hat / (jnp.sqrt(second_hat) + adam_epsilon) + d...  6.78 us
  transfers between devices with their start and end apart: 4, of which 3 were waited for; matrix products, arithmetic and copies ran while one was open for 1% of the time, Pallas kernels for 0%

profile of v2, /device:TPU:0, one launch (start us, length us, event | category | flops | bytes accessed | tf_op | source)
XLA Modules:
  0.0 232.7 jit_solution(14624408138977699593)
XLA Ops:
  0.7 1.3 fusion.21
  2.0 1.3 fusion.22
  4.6 1.2 multiply_sine_fusion
  5.9 1.3 copy-done.1
  10.3 59.1 %gather_weights.1 = (bf16[640,1536]{1,0:T(8,128)(2,1)S(1)}, bf16[1024,640]{1,0:T(8,128)(2,1)S(1)}, bf16[640,4096]{1,0:T(8,128)(2,1)}, bf16[2048,640]{1,0:T(8,128)(2,1)}) custom-call(bf16[160,1536]{1,0:T(8,128)(2,1)S(1)} %copy-done.3, bf16[256,640]{1,0:T(8,128)(2,1)S(1)} %copy-done.4, bf16[160,4096]{1,0:T(8,128)(2,1)S(1)} %copy-done.1, ...), custom_call_target="tpu_custom_call" | custom-call | bytes 25000000 | tf_op jit(solution)/shard_map/gather_weights/pallas_call | solution.py:213
  69.4 1.3 copy-done
  71.8 3.9 %before_attention.1 = (bf16[640,256]{1,0:T(8,128)(2,1)}, f32[256,1536]{1,0:T(8,128)}, bf16[256,1024]{1,0:T(8,128)(2,1)}, bf16[256,512]{1,0:T(8,128)(2,1)}) custom-call(bf16[256,640]{1,0:T(8,128)(2,1)} %hidden.5, bf16[640,1536]{1,0:T(8,128)(2,1)} %copy-done, f32[1,640]{1,0:T(1,128)} %get-tuple-element.98.gain_in, f32[1,256]{1,0:T(1,128)} %get-tuple-element.100.gain_q, ...), custom_call_target="tpu_custom_call" | custom-call | flops 503316480 | bytes 10000000 | tf_op jit(solution)/shard_map/before_attention/pallas_call | solution.py:593
  76.8 2.5 %collective-permute-start = (bf16[256,640]{1,0:T(8,128)(2,1)S(1)}, bf16[256,640]{1,0:T(8,128)(2,1)S(1)}, u32[]{:S(2)}, u32[]{:S(2)}) collective-permute-start(bf16[256,640]{1,0:T(8,128)(2,1)S(1)} %pad_maximum_fusion), channel_id=1, source_target_pairs={{0,2},{1,3},{2,4},{3,5},{4,6},{5,7},{6,8},{7,9},{8,10},{9,11},{10,... | collective-permute-start | bytes 983048 | tf_op jit(solution)/shard_map/ppermute | solution.py:33
  79.3 2.2 collective-permute-start.1
  82.2 5.0 %collective-permute-done = bf16[256,640]{1,0:T(8,128)(2,1)S(1)} collective-permute-done((bf16[256,640]{1,0:T(8,128)(2,1)S(1)}, bf16[256,640]{1,0:T(8,128)(2,1)S(1)}, u32[]{:S(2)}, u32[]{:S(2)}) %collective-permute-start) | collective-permute-done | bytes 327712 | tf_op jit(solution)/shard_map/ppermute | solution.py:33
  90.0 25.2 %attention_and_ffn.1 = (bf16[256,640]{1,0:T(8,128)(2,1)}, bf16[256,1024]{1,0:T(8,128)(2,1)}, bf16[640,256]{1,0:T(8,128)(2,1)}, bf16[256,2048]{1,0:T(8,128)(2,1)}...) custom-call(bf16[256,640]{1,0:T(8,128)(2,1)} %hidden.5, ...), custom_call_target="tpu_custom_call" | custom-call | flops 8000000000 | bytes 10000000 | tf_op jit(solution)/shard_map/attention_and_ffn/pallas_call | solution.py:593
  115.2 1.5 convert.27
  116.8 1.3 collective-permute-start.2
  118.1 1.5 collective-permute-start.3
  121.8 1.1 collective-permute-done.2
  122.9 11.3 %collective-permute-done.3 = bf16[256,512]{1,0:T(8,128)(2,1)S(1)} collective-permute-done((bf16[256,512]{1,0:T(8,128)(2,1)S(1)}, bf16[256,512]{1,0:T(8,128)(2,1)S(1)}, u32[]{:S(2)}, u32[]{:S(2)}) %collective-permute-start.3) | collective-permute-done | bytes 262176 | tf_op jit(solution)/shard_map/ppermute | solution.py:33
  134.3 1.9 convert_add_fusion.d_own
  136.2 5.0 %after_attention.1 = (bf16[256,1536]{1,0:T(8,128)(2,1)}, bf16[256,640]{1,0:T(8,128)(2,1)}, f32[1,640]{1,0:T(1,128)}, f32[1,256]{1,0:T(1,128)}, f32[1,256]{1,0:T(1,128)}) custom-call(bf16[256,640]{1,0:T(8,128)(2,1)} %hidden.5, bf16[640,1536]{1,0:T(8,128)(2,1)} %copy-done, f32[1,640]{1,0:T(1,128)} %get-tuple-element.98.gain_in, ...), custom_call_target="tpu_custom_call" | custom-call | flops 503316480 | bytes 10000000 | tf_op jit(solution)/shard_map/after_attention/pallas_call | solution.py:593
  143.5 1.4 copy.39
  146.0 1.5 copy.44.refs_1_
  149.5 74.2 %sum_gradients.1 = (f32[160,256]{1,0:T(8,128)S(1)}, f32[160,512]{1,0:T(8,128)S(1)}, f32[80,256]{1,0:T(8,128)S(1)}, f32[80,512]{1,0:T(8,128)S(1)}, f32[16,128]{1,0:T(8,128)S(1)}) custom-call(bf16[640,256]{1,0:T(8,128)(2,1)S(1)} %copy-done.6, bf16[256,2048]{1,0:T(8,128)(2,1)S(1)} %copy.44.refs_1_, bf16[640,256]{1,0:T(8,128)(2,1)S(1)} %copy-done.9, ...), custom_call_target="tpu_custom_call" | custom-call | flops 3000000000 | bytes 12000000 | tf_op jit(solution)/shard_map/sum_gradients/pallas_call | solution.py:410
  223.8 2.2 convert_subtract_fusion
  227.6 1.8 convert_subtract_fusion.2
  229.3 1.3 multiply_subtract_fusion
  (82 shorter events, 21.4 us)
Async XLA Ops:
  5.9 1.3 copy-start.1
  69.4 1.3 copy-start
  76.8 12.5 %copy-start.12 = (bf16[256,512]{1,0:T(8,128)(2,1)S(1)}, bf16[256,512]{1,0:T(8,128)(2,1)}, u32[]{:S(2)}) copy-start(bf16[256,512]{1,0:T(8,128)(2,1)} %get-tuple-element.50) | copy-start | bytes 786436
  76.8 10.4 %collective-permute-start = (bf16[256,640]{1,0:T(8,128)(2,1)S(1)}, bf16[256,640]{1,0:T(8,128)(2,1)S(1)}, u32[]{:S(2)}, u32[]{:S(2)}) collective-permute-start(bf16[256,640]{1,0:T(8,128)(2,1)S(1)} %pad_maximum_fusion), channel_id=1, source_target_pairs={{0,2},{1,3},{2,4},{3,5},{4,6},{5,7},{6,8},{7,9},{8,10},{9,11},{10,... | collective-permute-start | bytes 983048 | tf_op jit(solution)/shard_map/ppermute | solution.py:33
  79.3 8.0 %collective-permute-start.1 = (bf16[256,640]{1,0:T(8,128)(2,1)S(1)}, bf16[256,640]{1,0:T(8,128)(2,1)S(1)}, u32[]{:S(2)}, u32[]{:S(2)}) collective-permute-start(bf16[256,640]{1,0:T(8,128)(2,1)S(1)} %pad_maximum_fusion), channel_id=1, source_target_pairs={{0,1},{1,2},{2,3},{3,4},{4,5},{5,6},{6,7},{7,8},{8,9},{9,10},{10,1... | collective-permute-start | bytes 983048 | tf_op jit(solution)/shard_map/ppermute | solution.py:33
  116.8 6.2 %collective-permute-start.2 = (bf16[256,512]{1,0:T(8,128)(2,1)S(1)}, bf16[256,512]{1,0:T(8,128)(2,1)S(1)}, u32[]{:S(2)}, u32[]{:S(2)}) collective-permute-start(bf16[256,512]{1,0:T(8,128)(2,1)S(1)} %get-tuple-element.93), channel_id=1, source_target_pairs={{1,0},{2,1},{3,2},{4,3},{5,4},{6,5},{7,6},{8,7},{9,8},{10,9},{11,1... | collective-permute-start | bytes 786440 | tf_op jit(solution)/shard_map/ppermute | solution.py:33
  118.1 16.2 %collective-permute-start.3 = (bf16[256,512]{1,0:T(8,128)(2,1)S(1)}, bf16[256,512]{1,0:T(8,128)(2,1)S(1)}, u32[]{:S(2)}, u32[]{:S(2)}) collective-permute-start(bf16[256,512]{1,0:T(8,128)(2,1)S(1)} %get-tuple-element.94), channel_id=1, source_target_pairs={{2,0},{3,1},{4,2},{5,3},{6,4},{7,5},{8,6},{9,7},{10,8},{11,9},{12,... | collective-permute-start | bytes 786440 | tf_op jit(solution)/shard_map/ppermute | solution.py:33
  136.2 5.7 %copy-start.23 = (f32[1,640]{1,0:T(1,128)S(1)}, f32[1,640]{1,0:T(1,128)}, u32[]{:S(2)}) copy-start(f32[1,640]{1,0:T(1,128)} %get-tuple-element.69) | copy-start | bytes 7684
  136.2 5.7 %copy-start.22 = (f32[1,640]{1,0:T(1,128)S(1)}, f32[1,640]{1,0:T(1,128)}, u32[]{:S(2)}) copy-start(f32[1,640]{1,0:T(1,128)} %get-tuple-element.70) | copy-start | bytes 7684
  136.2 5.7 %copy-start.21 = (f32[1,640]{1,0:T(1,128)S(1)}, f32[1,640]{1,0:T(1,128)}, u32[]{:S(2)}) copy-start(f32[1,640]{1,0:T(1,128)} %get-tuple-element.71) | copy-start | bytes 7684
  144.9 2.6 %copy-start.6 = (bf16[640,256]{1,0:T(8,128)(2,1)S(1)}, bf16[640,256]{1,0:T(8,128)(2,1)}, u32[]{:S(2)}) copy-start(bf16[640,256]{1,0:T(8,128)(2,1)} %get-tuple-element.60.refs_0_) | copy-start | bytes 983044
  144.9 2.6 %copy-start.7 = (bf16[256,2048]{1,0:T(8,128)(2,1)S(1)}, bf16[256,2048]{1,0:T(8,128)(2,1)}, u32[]{:S(2)}) copy-start(bf16[256,2048]{1,0:T(8,128)(2,1)} %get-tuple-element.67.refs_7_) | copy-start | bytes 3145732
  144.9 2.6 %copy-start.8 = (bf16[256,1024]{1,0:T(8,128)(2,1)S(1)}, bf16[256,1024]{1,0:T(8,128)(2,1)}, u32[]{:S(2)}) copy-start(bf16[256,1024]{1,0:T(8,128)(2,1)} %get-tuple-element.65.refs_5_) | copy-start | bytes 1572868
  144.9 2.6 %copy-start.9 = (bf16[640,256]{1,0:T(8,128)(2,1)S(1)}, bf16[640,256]{1,0:T(8,128)(2,1)}, u32[]{:S(2)}) copy-start(bf16[640,256]{1,0:T(8,128)(2,1)} %get-tuple-element.62.refs_2_) | copy-start | bytes 983044
  149.5 74.3 %copy-start.13 = (f32[160,512]{1,0:T(8,128)S(1)}, f32[160,512]{1,0:T(8,128)}, u32[]{:S(2)}) copy-start(f32[160,512]{1,0:T(8,128)} %param.30) | copy-start | bytes 983044
  149.5 74.3 %copy-start.14 = (f32[160,512]{1,0:T(8,128)S(1)}, f32[160,512]{1,0:T(8,128)}, u32[]{:S(2)}) copy-start(f32[160,512]{1,0:T(8,128)} %param.35) | copy-start | bytes 983044
  149.5 76.5 %copy-start.15 = (f32[512,80]{0,1:T(8,128)S(1)}, f32[512,80]{0,1:T(8,128)}, u32[]{:S(2)}) copy-start(f32[512,80]{0,1:T(8,128)} %param.31) | copy-start | bytes 491524
  149.5 76.5 %copy-start.16 = (f32[512,80]{0,1:T(8,128)S(1)}, f32[512,80]{0,1:T(8,128)}, u32[]{:S(2)}) copy-start(f32[512,80]{0,1:T(8,128)} %param.36) | copy-start | bytes 491524
  223.7 3.1 %copy-start.19 = (f32[256,80]{0,1:T(8,128)S(1)}, f32[256,80]{0,1:T(8,128)}, u32[]{:S(2)}) copy-start(f32[256,80]{0,1:T(8,128)} %param.29) | copy-start | bytes 245764
  223.7 3.1 %copy-start.20 = (f32[256,80]{0,1:T(8,128)S(1)}, f32[256,80]{0,1:T(8,128)}, u32[]{:S(2)}) copy-start(f32[256,80]{0,1:T(8,128)} %param.34) | copy-start | bytes 245764
  223.8 3.8 %copy-start.17 = (f32[160,192]{1,0:T(8,128)S(1)}, f32[160,192]{1,0:T(8,128)}, u32[]{:S(2)}) copy-start(f32[160,192]{1,0:T(8,128)} %param.28) | copy-start | bytes 368644
  223.8 3.8 %copy-start.18 = (f32[160,192]{1,0:T(8,128)S(1)}, f32[160,192]{1,0:T(8,128)}, u32[]{:S(2)}) copy-start(f32[160,192]{1,0:T(8,128)} %param.33) | copy-start | bytes 368644
  223.8 5.5 %copy-start.24 = (f32[96]{0:T(128)S(1)}, f32[96]{0:T(128)}, u32[]{:S(2)}) copy-start(f32[96]{0:T(128)} %param.32) | copy-start | bytes 1156
  223.8 5.5 %copy-start.25 = (f32[96]{0:T(128)S(1)}, f32[96]{0:T(128)}, u32[]{:S(2)}) copy-start(f32[96]{0:T(128)} %param.37) | copy-start | bytes 1156
  (6 other events, 6.1 us)

commit v3 on v2

--- a/solution.py
+++ b/solution.py
@@ -175,7 +175,7 @@
         part = place(which, lax.rem(g + groups - far, groups), index)
         send(part, part, b_send.at[item, slot], b_recv.at[item, slot], (g, mate)).wait_recv()
 
-    for turn in range(len(items) + 2):
+    for turn in range(len(items) + 5):
         if turn < len(items):
             which, far = items[turn]
             part = place(which, lax.rem(g + groups - far, groups), r)
@@ -185,12 +185,12 @@
             push(turn, 0, r, one)
             push(turn, 1, r, two)
             push(turn, 3, r, mate)
-        item = turn - 1
+        item = turn - 2
         if 0 <= item < len(items):
             arrived(item, 0, one)
             push(item, 2, one, two)
             push(item, 4, one, mate)
-        item = turn - 2
+        item = turn - 5
         if 0 <= item < len(items):
             arrived(item, 1, two)
             push(item, 5, two, mate)
@@ -352,15 +352,14 @@
             far_copy(stage).start()
 
     meet(g, r, mate, one, two, groups)
-    for turn in range(groups + 3):
+    for turn in range(groups + 2):
         if turn < groups:
             make(turn)
+            pass_one(turn)
         if 0 <= turn - 1 < groups:
-            pass_one(turn - 1)
+            pass_two(turn - 1)
         if 0 <= turn - 2 < groups:
-            pass_two(turn - 2)
-        if 0 <= turn - 3 < groups:
-            pass_far(turn - 3)
+            pass_far(turn - 2)
     for stage in range(groups - 1):
         far_copy(stage).wait_recv()
     at_row = 0
@@ -451,7 +450,11 @@
     return rope_apply(norm_apply(values, gain), cosine, sine)
 
 
-def before_kernel(hidden, w_qkv, gain_in, gain_q, gain_k, cosine, sine, attn_in_t, raw, query, keyval):
+def before_kernel(
+    hidden, w_qkv, gain_in, gain_q, gain_k, cosine, sine, ids, attn_in_t, raw, query, keyval
+):
+    marks = (ids[...] + 1).astype(jnp.float32)
+    keyval[:, 2 * HD :] = low(jnp.broadcast_to(marks, (marks.shape[0], lanes)))
     attn_in = norm_apply(hidden[...].astype(jnp.float32), gain_in[...])
     attn_in_t[...] = low(attn_in.T)
     attn_in = low(attn_in)
@@ -465,22 +468,32 @@
         elif head == H:
             keyval[:, :HD] = low(rotate_norm(part, gain_k[...], cos, sin))
         else:
-            keyval[:, HD:] = low(part)
-
-
-def middle_kernel(
-    hidden, cotangent, query, keys, values, own_ids, key_ids, w_out, w_gate_up, w_down,
-    gain_attn_out, gain_ffn_in, gain_ffn_out,
-    block_out, mixed, ffn_in_t, act, d_down_t, d_gate_up, d_proj_t, d_query, d_keyval, d_residual,
-    g_attn_out, g_ffn_in, g_ffn_out,
-    bias, probs, gate_up, d_mixed, total,
-):
+            keyval[:, HD : 2 * HD] = low(part)
+
+
+def middle_kernel(reaches, *refs):
+    parts, refs = refs[: reaches + 1], refs[reaches + 1 :]
+    (hidden, cotangent, query, w_out, w_gate_up, w_down, gain_attn_out, gain_ffn_in, gain_ffn_out) = refs[:9]
+    d_parts, refs = refs[9 : 10 + reaches], refs[10 + reaches :]
+    (
+        block_out, mixed, ffn_in_t, act, d_down_t, d_gate_up, d_proj_t, d_query, d_residual,
+        g_attn_out, g_ffn_in, g_ffn_out,
+        bias, probs, gate_up, d_mixed, total, keys, values, d_keyval,
+    ) = refs
     tokens = hidden.shape[0]
     span = keys.shape[0]
+    marks = []
+    for at, part in enumerate(parts):
+        here = slice(at * tokens, (at + 1) * tokens)
+        keys[here, :] = part[:, :HD]
+        values[here, :] = part[:, HD : 2 * HD]
+        marks.append(part[:, 2 * HD :].astype(jnp.float32))
+    key_ids = jnp.concatenate([mark.T[:1, :] for mark in marks], axis=1)
+    own_ids = marks[-1][:, :1]
     scaling = HD ** (-0.5)
     row = lax.broadcasted_iota(jnp.int32, (tokens, span), 0) + (span - tokens)
     gap = row - lax.broadcasted_iota(jnp.int32, (tokens, span), 1)
-    allowed = (own_ids[...] == key_ids[...]) & (gap >= 0) & (gap < WINDOW)
+    allowed = (own_ids == key_ids) & (gap >= 0) & (gap < WINDOW)
     bias[...] = jnp.where(allowed, 0.0, neg_fill)
 
     def head_columns(head):
@@ -562,27 +575,40 @@
         return carry
 
     lax.fori_loop(0, H, attend_back, 0)
-
-
-def after_kernel(
-    hidden, w_qkv, gain_in, gain_q, gain_k, cosine, sine, raw, d_query, d_own, d_residual,
-    d_qkv, grad_in, g_in, g_q, g_k,
-):
+    for at, part in enumerate(d_parts):
+        part[...] = d_keyval[at * tokens : (at + 1) * tokens, :].astype(part.dtype)
+
+
+def after_query_kernel(w_query, gain_q, cosine, sine, raw, d_query, d_low, d_attn_in, g_q):
     cos, sin = cosine[...], sine[...]
     sums = None
-    for head in range(H + 1):
+    for head in range(H):
         here = slice(head * HD, (head + 1) * HD)
-        gain = gain_q if head < H else gain_k
-        unused, pull = jax.vjp(lambda v, w: rotate_norm(v, w, cos, sin), raw[:, here], gain[...])
-        d_raw, d_gain = pull(d_query[:, here] if head < H else d_own[:, :HD])
-        d_qkv[:, here] = low(d_raw)
-        if head < H:
-            sums = d_gain if sums is None else sums + d_gain
-        else:
-            g_k[...] = d_gain
+        unused, pull = jax.vjp(lambda v, w: rotate_norm(v, w, cos, sin), raw[:, here], gain_q[...])
+        d_raw, d_gain = pull(d_query[:, here])
+        d_low[:, here] = low(d_raw)
+        sums = d_gain if sums is None else sums + d_gain
     g_q[...] = sums
-    d_qkv[:, (H + 1) * HD :] = low(d_own[:, HD:])
-    d_attn_in = back_dot(d_qkv[...], w_qkv[...])
+    d_attn_in[...] = back_dot(d_low[...], w_query[:, : H * HD])
+
+
+def after_key_kernel(reaches, *refs):
+    came, refs = refs[:reaches], refs[reaches:]
+    (
+        hidden, w_qkv, gain_in, gain_k, cosine, sine, raw, d_own, d_query_low, d_attn_query, d_residual,
+        d_qkv, grad_in, g_in, g_k,
+    ) = refs
+    d_keyval = d_own[...]
+    for part in came:
+        d_keyval = d_keyval + part[...].astype(jnp.float32)
+    cos, sin = cosine[...], sine[...]
+    at_key = slice(H * HD, (H + 1) * HD)
+    unused, pull = jax.vjp(lambda v, w: rotate_norm(v, w, cos, sin), raw[:, at_key], gain_k[...])
+    d_raw, g_k[...] = pull(d_keyval[:, :HD])
+    d_qkv[:, : H * HD] = d_query_low[...]
+    d_qkv[:, at_key] = low(d_raw)
+    d_qkv[:, (H + 1) * HD :] = low(d_keyval[:, HD:])
+    d_attn_in = d_attn_query[...] + back_dot(d_qkv[:, H * HD :], w_qkv[:, H * HD :])
     unused, pull = jax.vjp(norm_apply, hidden[...].astype(jnp.float32), gain_in[...])
     d_inputs, g_in[...] = pull(d_attn_in)
     grad_in[...] = low(d_residual[...] + d_inputs)
@@ -615,49 +641,53 @@
     gain_key = gains[:, 4 * D + HD : 4 * D + 2 * HD]
     cosine, sine = rope_tables(positions, HD)
     wide = (H + 2) * HD
-    attn_in_t, raw, query, keyval = plain_call(
+    attn_in_t, raw, query, moved = plain_call(
         before_kernel, "before_attention", 2 * tokens * D * wide,
-        [((D, tokens), b16), ((tokens, wide), f32), ((tokens, H * HD), b16), ((tokens, 2 * HD), b16)],
-        [], hidden_in, full_qkv, gain_attn_in, gain_query, gain_key, cosine, sine,
+        [((D, tokens), b16), ((tokens, wide), f32), ((tokens, H * HD), b16), ((tokens, 2 * HD + lanes), b16)],
+        [], hidden_in, full_qkv, gain_attn_in, gain_query, gain_key, cosine, sine, segment_ids[:, None],
     )
     reaches = -(-WINDOW // tokens)
-    marks = jnp.broadcast_to((segment_ids + 1).astype(b16)[:, None], (tokens, lanes))
-    moved = jnp.concatenate([keyval, marks], axis=1)
     parts = [moved]
     for reach in range(1, reaches + 1):
         parts.insert(0, shifted(moved, ("group", "replica"), reach))
     span = (reaches + 1) * tokens
-    every = jnp.concatenate(parts, axis=0)
-    key_ids = every[:, 2 * HD].astype(jnp.int32)[None, :]
-    own_ids = (segment_ids + 1)[:, None]
     gain_out = ((1, D), f32)
-    (
-        block_out, mixed, ffn_in_t, act, d_down_t, d_gate_up, d_proj_t, d_query, d_keyval, d_residual,
-        g_attn_out, g_ffn_in, g_ffn_out,
-    ) = plain_call(
-        middle_kernel, "attention_and_ffn", 8000000000,
-        [
+    done = plain_call(
+        functools.partial(middle_kernel, reaches), "attention_and_ffn", 8000000000,
+        [((tokens, 2 * HD), b16)] * reaches + [
+            ((tokens, 2 * HD), f32),
             ((tokens, D), b16), ((tokens, H * HD), b16), ((D, tokens), b16), ((tokens, FF), b16),
             ((D, tokens), b16), ((tokens, 2 * FF), b16), ((D, tokens), b16), ((tokens, H * HD), f32),
-            ((span, 2 * HD), f32), ((tokens, D), f32), gain_out, gain_out, gain_out,
+            ((tokens, D), f32), gain_out, gain_out, gain_out,
         ],
         [
             pltpu.VMEM((tokens, span), f32), pltpu.VMEM((H, tokens, span), f32),
             pltpu.VMEM((tokens, 2 * FF), f32), pltpu.VMEM((tokens, H * HD), b16),
-            pltpu.VMEM((tokens, D), f32),
+            pltpu.VMEM((tokens, D), f32), pltpu.VMEM((span, HD), b16), pltpu.VMEM((span, HD), b16),
+            pltpu.VMEM((span, 2 * HD), f32),
         ],
-        hidden_in, cotangent, query, every[:, :HD], every[:, HD : 2 * HD], own_ids, key_ids,
+        *parts, hidden_in, cotangent, query,
         full_out, full_gate_up, full_down, gain_attn_out, gain_ffn_in, gain_ffn_out,
     )
-    d_own = d_keyval[reaches * tokens :]
-    for reach in range(1, reaches + 1):
-        piece = d_keyval[(reaches - reach) * tokens : (reaches - reach + 1) * tokens]
-        d_own = d_own + shifted(piece.astype(b16), ("group", "replica"), -reach).astype(f32)
-    d_qkv, grad_in, g_in, g_q, g_k = plain_call(
-        after_kernel, "after_attention", 2 * tokens * D * wide,
-        [((tokens, wide), b16), ((tokens, D), b16), gain_out, ((1, HD), f32), ((1, HD), f32)],
-        [], hidden_in, full_qkv, gain_attn_in, gain_query, gain_key, cosine, sine, raw, d_query, d_own,
-        d_residual,
+    d_parts, d_own = done[:reaches], done[reaches]
+    (
+        block_out, mixed, ffn_in_t, act, d_down_t, d_gate_up, d_proj_t, d_query, d_residual,
+        g_attn_out, g_ffn_in, g_ffn_out,
+    ) = done[reaches + 1 :]
+    came = [
+        shifted(d_parts[reaches - reach], ("group", "replica"), -reach)
+        for reach in range(1, reaches + 1)
+    ]
+    d_query_low, d_attn_query, g_q = plain_call(
+        after_query_kernel, "after_attention_query", 2 * tokens * D * H * HD,
+        [((tokens, H * HD), b16), ((tokens, D), f32), ((1, HD), f32)],
+        [], full_qkv, gain_query, cosine, sine, raw, d_query,
+    )
+    d_qkv, grad_in, g_in, g_k = plain_call(
+        functools.partial(after_key_kernel, reaches), "after_attention_key", 2 * tokens * D * 2 * HD,
+        [((tokens, wide), b16), ((tokens, D), b16), gain_out, ((1, HD), f32)],
+        [], *came, hidden_in, full_qkv, gain_attn_in, gain_key, cosine, sine, raw, d_own, d_query_low,
+        d_attn_query, d_residual,
     )
     gain_terms = jnp.concatenate([g_in, g_attn_out, g_ffn_in, g_ffn_out, g_q, g_k], axis=1)[0]
     return block_out, grad_in, (

time: 234 us -> 224 us (0.957)
  other arithmetic: 17.2 us -> 10.2 us
  waiting for transfers between devices: 17.4 us -> 14.3 us
  starting transfers between devices: 7.37 us -> 9.87 us
    pallas_call x3 -> x4, Pallas kernels: 34.1 us -> 38 us  [plain_call(): pl.pallas_call(kernel, out_shape=[jax.ShapeDtypeStruct(shape, kind) for s...]
    pallas_call x1, Pallas kernels: 59.1 us -> 55.6 us  [gather_weights(): pl.pallas_call(functools.partial(gather_kernel, groups, replicas), out_sh...]
    ppermute x4, waiting for transfers between devices: 17.4 us -> 14.3 us  [shifted(): return lax.ppermute(value, axis, pairs)]
    pallas_call x1, Pallas kernels: 74.2 us -> 71.3 us  [sum_gradients(): pl.pallas_call(functools.partial(sum_kernel, groups, replicas, dims), out...]
    add x2 -> x0, other arithmetic: 2.61 us -> none  [the longest x1 1.93 us: layer_grads(): d_own + shifted(piece.astype(b16), ('group', 'replica'), -reach).astype(f32)]
    ppermute x4, starting transfers between devices: 7.37 us -> 9.87 us  [shifted(): return lax.ppermute(value, axis, pairs)]
    unnamed x57 -> x65, local copies, waits for them, and re-layouts: 11 us -> 12.5 us
  transfers between devices with their start and end apart: 4 -> 4, of which waited for: 3 -> 2; matrix products, arithmetic and copies ran while one was open for 1% -> 1% of each run, Pallas kernels for 0% -> 2%
where the time goes in v3:
time: 224 us; the launch traced here: 223 us
  Pallas kernels  165 us (74%)
  local copies, waits for them, and re-layouts  22.7 us (10%)
  waiting for transfers between devices  14.3 us (6%)
  other arithmetic  10.2 us (5%)
  starting transfers between devices  9.87 us (4%)
    pallas_call x1, Pallas kernels, sum_gradients(): pl.pallas_call(functools.partial(sum_kernel, groups, replicas, dims), out...  71.3 us
    pallas_call x1, Pallas kernels, gather_weights(): pl.pallas_call(functools.partial(gather_kernel, groups, replicas), out_sh...  55.6 us
    pallas_call x4, Pallas kernels, plain_call(): pl.pallas_call(kernel, out_shape=[jax.ShapeDtypeStruct(shape, kind) for s...  38 us
    ppermute x4, waiting for transfers between devices, shifted(): return lax.ppermute(value, axis, pairs)  14.3 us
    unnamed x65, local copies, waits for them, and re-layouts  12.5 us
    ppermute x4, starting transfers between devices, shifted(): return lax.ppermute(value, axis, pairs)  9.87 us
    sub x5, other arithmetic, adam_step(): old - learn_rate * (first_hat / (jnp.sqrt(second_hat) + adam_epsilon) + d...  6.78 us
  transfers between devices with their start and end apart: 4, of which 2 were waited for; matrix products, arithmetic and copies ran while one was open for 1% of the time, Pallas kernels for 2%

profile of v3, /device:TPU:0, one launch (start us, length us, event | category | flops | bytes accessed | tf_op | source)
XLA Modules:
  0.0 223.0 jit_solution(2966886824463097689)
XLA Ops:
  0.7 1.3 fusion.18
  2.0 1.3 fusion.19
  4.0 1.5 copy.38.ids
  5.4 1.2 multiply_sine_fusion
  6.7 1.3 copy-done.1
  8.0 1.1 copy-done.2
  11.1 55.6 %gather_weights.1 = (bf16[640,1536]{1,0:T(8,128)(2,1)S(1)}, bf16[1024,640]{1,0:T(8,128)(2,1)S(1)}, bf16[640,4096]{1,0:T(8,128)(2,1)}, bf16[2048,640]{1,0:T(8,128)(2,1)}) custom-call(bf16[160,1536]{1,0:T(8,128)(2,1)S(1)} %copy-done.3, bf16[256,640]{1,0:T(8,128)(2,1)S(1)} %copy-done.4, bf16[160,4096]{1,0:T(8,128)(2,1)S(1)} %copy-done.1, ...), custom_call_target="tpu_custom_call" | custom-call | bytes 25000000 | tf_op jit(solution)/shard_map/gather_weights/pallas_call | solution.py:213
  66.7 1.3 copy-done
  69.1 4.0 %before_attention.1 = (bf16[640,256]{1,0:T(8,128)(2,1)}, f32[256,1536]{1,0:T(8,128)}, bf16[256,1024]{1,0:T(8,128)(2,1)}, bf16[256,640]{1,0:T(8,128)(2,1)}) custom-call(bf16[256,640]{1,0:T(8,128)(2,1)} %refs_2_.3, bf16[640,1536]{1,0:T(8,128)(2,1)} %copy-done, f32[1,640]{1,0:T(1,128)} %get-tuple-element.102.gain_in.refs_4_, ...), custom_call_target="tpu_custom_call" | custom-call | flops 503316480 | bytes 10000000 | tf_op jit(solution)/shard_map/before_attention/pallas_call | solution.py:619
  73.0 5.0 %collective-permute-start = (bf16[256,640]{1,0:T(8,128)(2,1)}, bf16[256,640]{1,0:T(8,128)(2,1)S(1)}, u32[]{:S(2)}, u32[]{:S(2)}) collective-permute-start(bf16[256,640]{1,0:T(8,128)(2,1)} %get-tuple-element.53.refs_2_), channel_id=1, source_target_pairs={{0,2},{1,3},{2,4},{3,5},{4,6},{5,7},{6,8},{7,9},{8,10},{9,11},{10,... | collective-permute-start | bytes 983048 | tf_op jit(solution)/shard_map/ppermute | solution.py:33
  78.0 2.2 collective-permute-start.1
  80.2 6.1 %collective-permute-done.refs_0_ = bf16[256,640]{1,0:T(8,128)(2,1)S(1)} collective-permute-done((bf16[256,640]{1,0:T(8,128)(2,1)}, bf16[256,640]{1,0:T(8,128)(2,1)S(1)}, u32[]{:S(2)}, u32[]{:S(2)}) %collective-permute-start) | collective-permute-done | bytes 327712 | tf_op jit(solution)/shard_map/ppermute | solution.py:33
  87.1 25.0 %attention_and_ffn.1 = (bf16[256,512]{1,0:T(8,128)(2,1)}, bf16[256,512]{1,0:T(8,128)(2,1)}, f32[256,512]{1,0:T(8,128)}, bf16[256,640]{1,0:T(8,128)(2,1)}, bf16[2...) custom-call(bf16[256,640]{1,0:T(8,128)(2,1)} %copy-done.28, ...), custom_call_target="tpu_custom_call" | custom-call | flops 8000000000 | bytes 10000000 | tf_op jit(solution)/shard_map/attention_and_ffn/pallas_call | solution.py:619
  112.2 1.3 collective-permute-start.2
  113.5 1.5 collective-permute-start.3
  117.2 4.3 %after_attention_query.1 = (bf16[256,1024]{1,0:T(8,128)(2,1)}, f32[256,640]{1,0:T(8,128)}, f32[1,256]{1,0:T(1,128)}) custom-call(bf16[640,1536]{1,0:T(8,128)(2,1)} %copy-done, f32[1,256]{1,0:T(1,128)} %get-tuple-element.104.gain_q, f32[256,128]{1,0:T(8,128)} %get-tuple-element.106.cosine.refs_6_, f32[256,128]{1,0:T(8,128)} %get-tuple-element.105.sine.refs_7_, ...), custom_call_target="tpu_custom_call" | custom-call | flops 335544320 | bytes 10000000 | tf_op jit(solution)/shard_map/after_attention_query/pallas_call | solution.py:619
  121.5 8.1 %collective-permute-done.3.refs_1_ = bf16[256,512]{1,0:T(8,128)(2,1)S(1)} collective-permute-done((bf16[256,512]{1,0:T(8,128)(2,1)}, bf16[256,512]{1,0:T(8,128)(2,1)S(1)}, u32[]{:S(2)}, u32[]{:S(2)}) %collective-permute-start.3) | collective-permute-done | bytes 262176 | tf_op jit(solution)/shard_map/ppermute | solution.py:33
  130.3 4.7 %after_attention_key.1 = (bf16[256,1536]{1,0:T(8,128)(2,1)}, bf16[256,640]{1,0:T(8,128)(2,1)}, f32[1,640]{1,0:T(1,128)}, f32[1,256]{1,0:T(1,128)}) custom-call(bf16[256,512]{1,0:T(8,128)(2,1)} %copy-done.14, bf16[256,512]{1,0:T(8,128)(2,1)} %copy-done.15, bf16[256,640]{1,0:T(8,128)(2,1)} %refs_2_.3, bf16[640,1536]{1,0:T(8,128)(2,1)} %copy-done, ...), custom_call_target="tpu_custom_call" | custom-call | flops 167772160 | bytes 10000000 | tf_op jit(solution)/shard_map/after_attention_key/pallas_call | solution.py:619
  136.7 1.4 copy.39
  139.2 1.5 copy.44.refs_1_
  142.7 71.3 %sum_gradients.1 = (f32[160,256]{1,0:T(8,128)S(1)}, f32[160,512]{1,0:T(8,128)S(1)}, f32[80,256]{1,0:T(8,128)S(1)}, f32[80,512]{1,0:T(8,128)S(1)}, f32[16,128]{1,0:T(8,128)S(1)}) custom-call(bf16[640,256]{1,0:T(8,128)(2,1)S(1)} %copy-done.6, bf16[256,2048]{1,0:T(8,128)(2,1)S(1)} %copy.44.refs_1_, bf16[640,256]{1,0:T(8,128)(2,1)S(1)} %copy-done.9, ...), custom_call_target="tpu_custom_call" | custom-call | flops 3000000000 | bytes 12000000 | tf_op jit(solution)/shard_map/sum_gradients/pallas_call | solution.py:409
  214.2 2.2 convert_subtract_fusion
  217.9 1.8 convert_subtract_fusion.2
  219.7 1.3 multiply_subtract_fusion
  (81 shorter events, 15.8 us)
Async XLA Ops:
  6.7 1.3 copy-start.1
  73.0 13.3 %collective-permute-start = (bf16[256,640]{1,0:T(8,128)(2,1)}, bf16[256,640]{1,0:T(8,128)(2,1)S(1)}, u32[]{:S(2)}, u32[]{:S(2)}) collective-permute-start(bf16[256,640]{1,0:T(8,128)(2,1)} %get-tuple-element.53.refs_2_), channel_id=1, source_target_pairs={{0,2},{1,3},{2,4},{3,5},{4,6},{5,7},{6,8},{7,9},{8,10},{9,11},{10,... | collective-permute-start | bytes 983048 | tf_op jit(solution)/shard_map/ppermute | solution.py:33
  78.0 8.3 %collective-permute-start.1 = (bf16[256,640]{1,0:T(8,128)(2,1)}, bf16[256,640]{1,0:T(8,128)(2,1)S(1)}, u32[]{:S(2)}, u32[]{:S(2)}) collective-permute-start(bf16[256,640]{1,0:T(8,128)(2,1)} %get-tuple-element.53.refs_2_), channel_id=1, source_target_pairs={{0,1},{1,2},{2,3},{3,4},{4,5},{5,6},{6,7},{7,8},{8,9},{9,10},{10,1... | collective-permute-start | bytes 983048 | tf_op jit(solution)/shard_map/ppermute | solution.py:33
  112.2 9.3 %collective-permute-start.2 = (bf16[256,512]{1,0:T(8,128)(2,1)}, bf16[256,512]{1,0:T(8,128)(2,1)S(1)}, u32[]{:S(2)}, u32[]{:S(2)}) collective-permute-start(bf16[256,512]{1,0:T(8,128)(2,1)} %get-tuple-element.59), channel_id=1, source_target_pairs={{1,0},{2,1},{3,2},{4,3},{5,4},{6,5},{7,6},{8,7},{9,8},{10,9},{11,1... | collective-permute-start | bytes 786440 | tf_op jit(solution)/shard_map/ppermute | solution.py:33
  113.5 16.2 %collective-permute-start.3 = (bf16[256,512]{1,0:T(8,128)(2,1)}, bf16[256,512]{1,0:T(8,128)(2,1)S(1)}, u32[]{:S(2)}, u32[]{:S(2)}) collective-permute-start(bf16[256,512]{1,0:T(8,128)(2,1)} %get-tuple-element.60), channel_id=1, source_target_pairs={{2,0},{3,1},{4,2},{5,3},{6,4},{7,5},{8,6},{9,7},{10,8},{11,9},{12,... | collective-permute-start | bytes 786440 | tf_op jit(solution)/shard_map/ppermute | solution.py:33
  121.5 8.1 %copy-start.14 = (bf16[256,512]{1,0:T(8,128)(2,1)}, bf16[256,512]{1,0:T(8,128)(2,1)S(1)}, u32[]{:S(2)}) copy-start(bf16[256,512]{1,0:T(8,128)(2,1)S(1)} %collective-permute-done.2.refs_0_) | copy-start | bytes 786436
  130.3 5.4 %copy-start.24 = (f32[1,640]{1,0:T(1,128)S(1)}, f32[1,640]{1,0:T(1,128)}, u32[]{:S(2)}) copy-start(f32[1,640]{1,0:T(1,128)} %get-tuple-element.77) | copy-start | bytes 7684
  130.3 5.4 %copy-start.23 = (f32[1,640]{1,0:T(1,128)S(1)}, f32[1,640]{1,0:T(1,128)}, u32[]{:S(2)}) copy-start(f32[1,640]{1,0:T(1,128)} %get-tuple-element.78) | copy-start | bytes 7684
  130.3 5.5 %copy-start.22 = (f32[1,640]{1,0:T(1,128)S(1)}, f32[1,640]{1,0:T(1,128)}, u32[]{:S(2)}) copy-start(f32[1,640]{1,0:T(1,128)} %get-tuple-element.79) | copy-start | bytes 7684
  130.3 5.5 %copy-start.25 = (f32[1,256]{1,0:T(1,128)S(1)}, f32[1,256]{1,0:T(1,128)}, u32[]{:S(2)}) copy-start(f32[1,256]{1,0:T(1,128)} %get-tuple-element.80) | copy-start | bytes 3076
  138.1 2.6 %copy-start.6 = (bf16[640,256]{1,0:T(8,128)(2,1)S(1)}, bf16[640,256]{1,0:T(8,128)(2,1)}, u32[]{:S(2)}) copy-start(bf16[640,256]{1,0:T(8,128)(2,1)} %get-tuple-element.68.refs_0_) | copy-start | bytes 983044
  138.1 2.6 %copy-start.7 = (bf16[256,2048]{1,0:T(8,128)(2,1)S(1)}, bf16[256,2048]{1,0:T(8,128)(2,1)}, u32[]{:S(2)}) copy-start(bf16[256,2048]{1,0:T(8,128)(2,1)} %get-tuple-element.75.refs_7_) | copy-start | bytes 3145732
  138.2 2.6 %copy-start.8 = (bf16[256,1024]{1,0:T(8,128)(2,1)S(1)}, bf16[256,1024]{1,0:T(8,128)(2,1)}, u32[]{:S(2)}) copy-start(bf16[256,1024]{1,0:T(8,128)(2,1)} %get-tuple-element.73.refs_5_) | copy-start | bytes 1572868
  138.2 2.6 %copy-start.9 = (bf16[640,256]{1,0:T(8,128)(2,1)S(1)}, bf16[640,256]{1,0:T(8,128)(2,1)}, u32[]{:S(2)}) copy-start(bf16[640,256]{1,0:T(8,128)(2,1)} %get-tuple-element.70.refs_2_) | copy-start | bytes 983044
  142.7 71.4 %copy-start.12 = (f32[160,512]{1,0:T(8,128)S(1)}, f32[160,512]{1,0:T(8,128)}, u32[]{:S(2)}) copy-start(f32[160,512]{1,0:T(8,128)} %param.30) | copy-start | bytes 983044
  142.7 71.4 %copy-start.13 = (f32[160,512]{1,0:T(8,128)S(1)}, f32[160,512]{1,0:T(8,128)}, u32[]{:S(2)}) copy-start(f32[160,512]{1,0:T(8,128)} %param.35) | copy-start | bytes 983044
  142.7 73.6 %copy-start.16 = (f32[512,80]{0,1:T(8,128)S(1)}, f32[512,80]{0,1:T(8,128)}, u32[]{:S(2)}) copy-start(f32[512,80]{0,1:T(8,128)} %param.31) | copy-start | bytes 491524
  142.7 73.6 %copy-start.17 = (f32[512,80]{0,1:T(8,128)S(1)}, f32[512,80]{0,1:T(8,128)}, u32[]{:S(2)}) copy-start(f32[512,80]{0,1:T(8,128)} %param.36) | copy-start | bytes 491524
  214.1 3.1 %copy-start.20 = (f32[256,80]{0,1:T(8,128)S(1)}, f32[256,80]{0,1:T(8,128)}, u32[]{:S(2)}) copy-start(f32[256,80]{0,1:T(8,128)} %param.29) | copy-start | bytes 245764
  214.1 3.1 %copy-start.21 = (f32[256,80]{0,1:T(8,128)S(1)}, f32[256,80]{0,1:T(8,128)}, u32[]{:S(2)}) copy-start(f32[256,80]{0,1:T(8,128)} %param.34) | copy-start | bytes 245764
  214.1 3.8 %copy-start.18 = (f32[160,192]{1,0:T(8,128)S(1)}, f32[160,192]{1,0:T(8,128)}, u32[]{:S(2)}) copy-start(f32[160,192]{1,0:T(8,128)} %param.28) | copy-start | bytes 368644
  214.1 3.8 %copy-start.19 = (f32[160,192]{1,0:T(8,128)S(1)}, f32[160,192]{1,0:T(8,128)}, u32[]{:S(2)}) copy-start(f32[160,192]{1,0:T(8,128)} %param.33) | copy-start | bytes 368644
  214.1 5.5 %copy-start.26 = (f32[96]{0:T(128)S(1)}, f32[96]{0:T(128)}, u32[]{:S(2)}) copy-start(f32[96]{0:T(128)} %param.32) | copy-start | bytes 1156
  214.2 5.5 %copy-start.27 = (f32[96]{0:T(128)S(1)}, f32[96]{0:T(128)}, u32[]{:S(2)}) copy-start(f32[96]{0:T(128)} %param.37) | copy-start | bytes 1156
  (10 other events, 9.6 us)

commit v4 on v3

--- a/solution.py
+++ b/solution.py
@@ -327,13 +327,17 @@
             return carry
 
         lax.fori_loop(0, 4, for_mate, 0)
-        lax.fori_loop(0, 4, for_me, 0)
+        lax.fori_loop(0, 2, for_me, 0)
+        pass_one(stage)
+        lax.fori_loop(2, 4, for_me, 0)
 
     def pass_one(stage):
         for m in (1, 0):
             mate_copy(stage, m).wait_recv()
             add(kept.at[stage, m], from_mate.at[stage, m])
             one_copy(stage, m).start()
+
+    def pass_rest(stage):
         for m in (2, 3):
             mate_copy(stage, m).wait_recv()
             add(kept.at[stage, m], from_mate.at[stage, m])
@@ -355,7 +359,7 @@
     for turn in range(groups + 2):
         if turn < groups:
             make(turn)
-            pass_one(turn)
+            pass_rest(turn)
         if 0 <= turn - 1 < groups:
             pass_two(turn - 1)
         if 0 <= turn - 2 < groups:

time: 224 us -> 224 us (level)
  no operation moved by 1% of the time
where the time goes in v4:
time: 224 us; the launch traced here: 223 us
  Pallas kernels  165 us (74%)
  local copies, waits for them, and re-layouts  22.7 us (10%)
  waiting for transfers between devices  14.3 us (6%)
  other arithmetic  10.2 us (5%)
  starting transfers between devices  9.87 us (4%)
    pallas_call x1, Pallas kernels, sum_gradients(): pl.pallas_call(functools.partial(sum_kernel, groups, replicas, dims), out...  71.4 us
    pallas_call x1, Pallas kernels, gather_weights(): pl.pallas_call(functools.partial(gather_kernel, groups, replicas), out_sh...  55.6 us
    pallas_call x4, Pallas kernels, plain_call(): pl.pallas_call(kernel, out_shape=[jax.ShapeDtypeStruct(shape, kind) for s...  38 us
    ppermute x4, waiting for transfers between devices, shifted(): return lax.ppermute(value, axis, pairs)  14.3 us
    unnamed x65, local copies, waits for them, and re-layouts  12.5 us
    ppermute x4, starting transfers between devices, shifted(): return lax.ppermute(value, axis, pairs)  9.87 us
    sub x5, other arithmetic, adam_step(): old - learn_rate * (first_hat / (jnp.sqrt(second_hat) + adam_epsilon) + d...  6.78 us
  transfers between devices with their start and end apart: 4, of which 2 were waited for; matrix products, arithmetic and copies ran while one was open for 1% of the time, Pallas kernels for 2%

profile of v4, /device:TPU:0, one launch (start us, length us, event | category | flops | bytes accessed | tf_op | source)
XLA Modules:
  0.0 223.0 jit_solution(18338107873244569754)
XLA Ops:
  0.7 1.3 fusion.18
  2.0 1.3 fusion.19
  4.0 1.5 copy.38.ids
  5.4 1.2 multiply_sine_fusion
  6.7 1.3 copy-done.1
  8.0 1.1 copy-done.2
  11.1 55.6 %gather_weights.1 = (bf16[640,1536]{1,0:T(8,128)(2,1)S(1)}, bf16[1024,640]{1,0:T(8,128)(2,1)S(1)}, bf16[640,4096]{1,0:T(8,128)(2,1)}, bf16[2048,640]{1,0:T(8,128)(2,1)}) custom-call(bf16[160,1536]{1,0:T(8,128)(2,1)S(1)} %copy-done.3, bf16[256,640]{1,0:T(8,128)(2,1)S(1)} %copy-done.4, bf16[160,4096]{1,0:T(8,128)(2,1)S(1)} %copy-done.1, ...), custom_call_target="tpu_custom_call" | custom-call | bytes 25000000 | tf_op jit(solution)/shard_map/gather_weights/pallas_call | solution.py:213
  66.7 1.3 copy-done
  69.1 4.0 %before_attention.1 = (bf16[640,256]{1,0:T(8,128)(2,1)}, f32[256,1536]{1,0:T(8,128)}, bf16[256,1024]{1,0:T(8,128)(2,1)}, bf16[256,640]{1,0:T(8,128)(2,1)}) custom-call(bf16[256,640]{1,0:T(8,128)(2,1)} %refs_2_.3, bf16[640,1536]{1,0:T(8,128)(2,1)} %copy-done, f32[1,640]{1,0:T(1,128)} %get-tuple-element.102.gain_in.refs_4_, ...), custom_call_target="tpu_custom_call" | custom-call | flops 503316480 | bytes 10000000 | tf_op jit(solution)/shard_map/before_attention/pallas_call | solution.py:623
  73.0 5.0 %collective-permute-start = (bf16[256,640]{1,0:T(8,128)(2,1)}, bf16[256,640]{1,0:T(8,128)(2,1)S(1)}, u32[]{:S(2)}, u32[]{:S(2)}) collective-permute-start(bf16[256,640]{1,0:T(8,128)(2,1)} %get-tuple-element.53.refs_2_), channel_id=1, source_target_pairs={{0,2},{1,3},{2,4},{3,5},{4,6},{5,7},{6,8},{7,9},{8,10},{9,11},{10,... | collective-permute-start | bytes 983048 | tf_op jit(solution)/shard_map/ppermute | solution.py:33
  78.0 2.2 collective-permute-start.1
  80.2 6.1 %collective-permute-done.refs_0_ = bf16[256,640]{1,0:T(8,128)(2,1)S(1)} collective-permute-done((bf16[256,640]{1,0:T(8,128)(2,1)}, bf16[256,640]{1,0:T(8,128)(2,1)S(1)}, u32[]{:S(2)}, u32[]{:S(2)}) %collective-permute-start) | collective-permute-done | bytes 327712 | tf_op jit(solution)/shard_map/ppermute | solution.py:33
  87.1 25.0 %attention_and_ffn.1 = (bf16[256,512]{1,0:T(8,128)(2,1)}, bf16[256,512]{1,0:T(8,128)(2,1)}, f32[256,512]{1,0:T(8,128)}, bf16[256,640]{1,0:T(8,128)(2,1)}, bf16[2...) custom-call(bf16[256,640]{1,0:T(8,128)(2,1)} %copy-done.28, ...), custom_call_target="tpu_custom_call" | custom-call | flops 8000000000 | bytes 10000000 | tf_op jit(solution)/shard_map/attention_and_ffn/pallas_call | solution.py:623
  112.2 1.3 collective-permute-start.2
  113.5 1.5 collective-permute-start.3
  117.2 4.3 %after_attention_query.1 = (bf16[256,1024]{1,0:T(8,128)(2,1)}, f32[256,640]{1,0:T(8,128)}, f32[1,256]{1,0:T(1,128)}) custom-call(bf16[640,1536]{1,0:T(8,128)(2,1)} %copy-done, f32[1,256]{1,0:T(1,128)} %get-tuple-element.104.gain_q, f32[256,128]{1,0:T(8,128)} %get-tuple-element.106.cosine.refs_6_, f32[256,128]{1,0:T(8,128)} %get-tuple-element.105.sine.refs_7_, ...), custom_call_target="tpu_custom_call" | custom-call | flops 335544320 | bytes 10000000 | tf_op jit(solution)/shard_map/after_attention_query/pallas_call | solution.py:623
  121.5 8.1 %collective-permute-done.3.refs_1_ = bf16[256,512]{1,0:T(8,128)(2,1)S(1)} collective-permute-done((bf16[256,512]{1,0:T(8,128)(2,1)}, bf16[256,512]{1,0:T(8,128)(2,1)S(1)}, u32[]{:S(2)}, u32[]{:S(2)}) %collective-permute-start.3) | collective-permute-done | bytes 262176 | tf_op jit(solution)/shard_map/ppermute | solution.py:33
  130.3 4.7 %after_attention_key.1 = (bf16[256,1536]{1,0:T(8,128)(2,1)}, bf16[256,640]{1,0:T(8,128)(2,1)}, f32[1,640]{1,0:T(1,128)}, f32[1,256]{1,0:T(1,128)}) custom-call(bf16[256,512]{1,0:T(8,128)(2,1)} %copy-done.14, bf16[256,512]{1,0:T(8,128)(2,1)} %copy-done.15, bf16[256,640]{1,0:T(8,128)(2,1)} %refs_2_.3, bf16[640,1536]{1,0:T(8,128)(2,1)} %copy-done, ...), custom_call_target="tpu_custom_call" | custom-call | flops 167772160 | bytes 10000000 | tf_op jit(solution)/shard_map/after_attention_key/pallas_call | solution.py:623
  136.7 1.4 copy.39
  139.2 1.5 copy.44.refs_1_
  142.7 71.4 %sum_gradients.1 = (f32[160,256]{1,0:T(8,128)S(1)}, f32[160,512]{1,0:T(8,128)S(1)}, f32[80,256]{1,0:T(8,128)S(1)}, f32[80,512]{1,0:T(8,128)S(1)}, f32[16,128]{1,0:T(8,128)S(1)}) custom-call(bf16[640,256]{1,0:T(8,128)(2,1)S(1)} %copy-done.6, bf16[256,2048]{1,0:T(8,128)(2,1)S(1)} %copy.44.refs_1_, bf16[640,256]{1,0:T(8,128)(2,1)S(1)} %copy-done.9, ...), custom_call_target="tpu_custom_call" | custom-call | flops 3000000000 | bytes 12000000 | tf_op jit(solution)/shard_map/sum_gradients/pallas_call | solution.py:413
  214.2 2.2 convert_subtract_fusion
  217.9 1.8 convert_subtract_fusion.2
  219.7 1.3 multiply_subtract_fusion
  (81 shorter events, 15.8 us)
Async XLA Ops:
  6.7 1.3 copy-start.1
  73.0 13.3 %collective-permute-start = (bf16[256,640]{1,0:T(8,128)(2,1)}, bf16[256,640]{1,0:T(8,128)(2,1)S(1)}, u32[]{:S(2)}, u32[]{:S(2)}) collective-permute-start(bf16[256,640]{1,0:T(8,128)(2,1)} %get-tuple-element.53.refs_2_), channel_id=1, source_target_pairs={{0,2},{1,3},{2,4},{3,5},{4,6},{5,7},{6,8},{7,9},{8,10},{9,11},{10,... | collective-permute-start | bytes 983048 | tf_op jit(solution)/shard_map/ppermute | solution.py:33
  78.0 8.3 %collective-permute-start.1 = (bf16[256,640]{1,0:T(8,128)(2,1)}, bf16[256,640]{1,0:T(8,128)(2,1)S(1)}, u32[]{:S(2)}, u32[]{:S(2)}) collective-permute-start(bf16[256,640]{1,0:T(8,128)(2,1)} %get-tuple-element.53.refs_2_), channel_id=1, source_target_pairs={{0,1},{1,2},{2,3},{3,4},{4,5},{5,6},{6,7},{7,8},{8,9},{9,10},{10,1... | collective-permute-start | bytes 983048 | tf_op jit(solution)/shard_map/ppermute | solution.py:33
  112.2 9.3 %collective-permute-start.2 = (bf16[256,512]{1,0:T(8,128)(2,1)}, bf16[256,512]{1,0:T(8,128)(2,1)S(1)}, u32[]{:S(2)}, u32[]{:S(2)}) collective-permute-start(bf16[256,512]{1,0:T(8,128)(2,1)} %get-tuple-element.59), channel_id=1, source_target_pairs={{1,0},{2,1},{3,2},{4,3},{5,4},{6,5},{7,6},{8,7},{9,8},{10,9},{11,1... | collective-permute-start | bytes 786440 | tf_op jit(solution)/shard_map/ppermute | solution.py:33
  113.5 16.2 %collective-permute-start.3 = (bf16[256,512]{1,0:T(8,128)(2,1)}, bf16[256,512]{1,0:T(8,128)(2,1)S(1)}, u32[]{:S(2)}, u32[]{:S(2)}) collective-permute-start(bf16[256,512]{1,0:T(8,128)(2,1)} %get-tuple-element.60), channel_id=1, source_target_pairs={{2,0},{3,1},{4,2},{5,3},{6,4},{7,5},{8,6},{9,7},{10,8},{11,9},{12,... | collective-permute-start | bytes 786440 | tf_op jit(solution)/shard_map/ppermute | solution.py:33
  121.5 8.1 %copy-start.14 = (bf16[256,512]{1,0:T(8,128)(2,1)}, bf16[256,512]{1,0:T(8,128)(2,1)S(1)}, u32[]{:S(2)}) copy-start(bf16[256,512]{1,0:T(8,128)(2,1)S(1)} %collective-permute-done.2.refs_0_) | copy-start | bytes 786436
  130.3 5.4 %copy-start.24 = (f32[1,640]{1,0:T(1,128)S(1)}, f32[1,640]{1,0:T(1,128)}, u32[]{:S(2)}) copy-start(f32[1,640]{1,0:T(1,128)} %get-tuple-element.77) | copy-start | bytes 7684
  130.3 5.4 %copy-start.23 = (f32[1,640]{1,0:T(1,128)S(1)}, f32[1,640]{1,0:T(1,128)}, u32[]{:S(2)}) copy-start(f32[1,640]{1,0:T(1,128)} %get-tuple-element.78) | copy-start | bytes 7684
  130.3 5.5 %copy-start.22 = (f32[1,640]{1,0:T(1,128)S(1)}, f32[1,640]{1,0:T(1,128)}, u32[]{:S(2)}) copy-start(f32[1,640]{1,0:T(1,128)} %get-tuple-element.79) | copy-start | bytes 7684
  130.3 5.5 %copy-start.25 = (f32[1,256]{1,0:T(1,128)S(1)}, f32[1,256]{1,0:T(1,128)}, u32[]{:S(2)}) copy-start(f32[1,256]{1,0:T(1,128)} %get-tuple-element.80) | copy-start | bytes 3076
  138.1 2.6 %copy-start.6 = (bf16[640,256]{1,0:T(8,128)(2,1)S(1)}, bf16[640,256]{1,0:T(8,128)(2,1)}, u32[]{:S(2)}) copy-start(bf16[640,256]{1,0:T(8,128)(2,1)} %get-tuple-element.68.refs_0_) | copy-start | bytes 983044
  138.1 2.6 %copy-start.7 = (bf16[256,2048]{1,0:T(8,128)(2,1)S(1)}, bf16[256,2048]{1,0:T(8,128)(2,1)}, u32[]{:S(2)}) copy-start(bf16[256,2048]{1,0:T(8,128)(2,1)} %get-tuple-element.75.refs_7_) | copy-start | bytes 3145732
  138.2 2.6 %copy-start.8 = (bf16[256,1024]{1,0:T(8,128)(2,1)S(1)}, bf16[256,1024]{1,0:T(8,128)(2,1)}, u32[]{:S(2)}) copy-start(bf16[256,1024]{1,0:T(8,128)(2,1)} %get-tuple-element.73.refs_5_) | copy-start | bytes 1572868
  138.2 2.6 %copy-start.9 = (bf16[640,256]{1,0:T(8,128)(2,1)S(1)}, bf16[640,256]{1,0:T(8,128)(2,1)}, u32[]{:S(2)}) copy-start(bf16[640,256]{1,0:T(8,128)(2,1)} %get-tuple-element.70.refs_2_) | copy-start | bytes 983044
  142.7 71.4 %copy-start.12 = (f32[160,512]{1,0:T(8,128)S(1)}, f32[160,512]{1,0:T(8,128)}, u32[]{:S(2)}) copy-start(f32[160,512]{1,0:T(8,128)} %param.30) | copy-start | bytes 983044
  142.7 71.5 %copy-start.13 = (f32[160,512]{1,0:T(8,128)S(1)}, f32[160,512]{1,0:T(8,128)}, u32[]{:S(2)}) copy-start(f32[160,512]{1,0:T(8,128)} %param.35) | copy-start | bytes 983044
  142.7 73.7 %copy-start.16 = (f32[512,80]{0,1:T(8,128)S(1)}, f32[512,80]{0,1:T(8,128)}, u32[]{:S(2)}) copy-start(f32[512,80]{0,1:T(8,128)} %param.31) | copy-start | bytes 491524
  142.7 73.7 %copy-start.17 = (f32[512,80]{0,1:T(8,128)S(1)}, f32[512,80]{0,1:T(8,128)}, u32[]{:S(2)}) copy-start(f32[512,80]{0,1:T(8,128)} %param.36) | copy-start | bytes 491524
  214.1 3.1 %copy-start.20 = (f32[256,80]{0,1:T(8,128)S(1)}, f32[256,80]{0,1:T(8,128)}, u32[]{:S(2)}) copy-start(f32[256,80]{0,1:T(8,128)} %param.29) | copy-start | bytes 245764
  214.1 3.1 %copy-start.21 = (f32[256,80]{0,1:T(8,128)S(1)}, f32[256,80]{0,1:T(8,128)}, u32[]{:S(2)}) copy-start(f32[256,80]{0,1:T(8,128)} %param.34) | copy-start | bytes 245764
  214.1 3.8 %copy-start.18 = (f32[160,192]{1,0:T(8,128)S(1)}, f32[160,192]{1,0:T(8,128)}, u32[]{:S(2)}) copy-start(f32[160,192]{1,0:T(8,128)} %param.28) | copy-start | bytes 368644
  214.1 3.8 %copy-start.19 = (f32[160,192]{1,0:T(8,128)S(1)}, f32[160,192]{1,0:T(8,128)}, u32[]{:S(2)}) copy-start(f32[160,192]{1,0:T(8,128)} %param.33) | copy-start | bytes 368644
  214.2 5.5 %copy-start.26 = (f32[96]{0:T(128)S(1)}, f32[96]{0:T(128)}, u32[]{:S(2)}) copy-start(f32[96]{0:T(128)} %param.32) | copy-start | bytes 1156
  214.2 5.5 %copy-start.27 = (f32[96]{0:T(128)S(1)}, f32[96]{0:T(128)}, u32[]{:S(2)}) copy-start(f32[96]{0:T(128)} %param.37) | copy-start | bytes 1156
  (10 other events, 9.6 us)
